TPU v7x, 256 devices: a whole 4x4x8 slice. The times are simulated.
256 devices in a mesh: ctx: 8 (over y, z_hi), chan: 32 (over z_lo, x, core).
Axes of the slice: x: 4, y: 4, z: 8 (z_hi: 2, z_lo: 4; z = z_hi * 4 + z_lo), core: 2. Of those that a mesh axis runs over, the one named last changes fastest.
Arguments:
- inputs: bfloat16 [2048, 131072], P('chan', 'ctx'), may hold values from -6 to 6
- mixed: bfloat16 [2048, 131072], P('chan', 'ctx'), may hold values from -6 to 6
- grad_out: bfloat16 [2048, 131072], P('chan', 'ctx'), may hold values from -6 to 6
- left_weight: bfloat16 [256, 512, 512], P(('ctx', 'chan')), may hold values from -0.25 to 0.25
- right_weight: bfloat16 [512, 256, 256], P(('ctx', 'chan')), may hold values from -0.375 to 0.375
- first_weight: bfloat16 [32, 64, 64], replicated, may hold values from -0.75 to 0.75
- second_weight: bfloat16 [64, 32, 32], replicated, may hold values from -1 to 1
Outputs:
- grad_input: bfloat16 [2048, 131072], P('chan', 'ctx')
- grad_left: bfloat16 [256, 512, 512], P(('ctx', 'chan'))
- grad_right: bfloat16 [512, 256, 256], P(('ctx', 'chan'))
- grad_first: float32 [32, 64, 64], replicated
- grad_second: float32 [64, 32, 32], replicated
All inputs are finite; a program needn't handle non-finite values.
Results may differ from a plain program's by a relative error of at most 0.0069.
Values may be sent and summed in bfloat16 or wider, within the bound.
A program may use at most 128 MiB of HBM per device.

v0:
```python
import jax
import jax.numpy as jnp
from jax import lax
from jax.sharding import PartitionSpec as P


def lower_part(weight):
    size = weight.shape[-1]
    rows = lax.broadcasted_iota(jnp.int32, (size, size), 0)
    cols = lax.broadcasted_iota(jnp.int32, (size, size), 1)
    return jnp.where(rows >= cols, weight, jnp.zeros_like(weight))


def spread(values, ranks, lanes):
    local_blocks, bsize, width = values.shape
    sectioned = values.reshape(1, 1, local_blocks, ranks, lanes, bsize // (ranks * lanes), width)
    sectioned = lax.all_to_all(sectioned, "chan", split_axis=4, concat_axis=1, tiled=True)
    sectioned = lax.all_to_all(sectioned, "ctx", split_axis=3, concat_axis=0, tiled=True)
    return sectioned.reshape(ranks * lanes * local_blocks, bsize // (ranks * lanes), width)


def gather_back(values, ranks, lanes):
    nblocks, positions, width = values.shape
    local_blocks = nblocks // (ranks * lanes)
    sectioned = values.reshape(ranks, lanes, local_blocks, 1, 1, positions, width)
    sectioned = lax.all_to_all(sectioned, "chan", split_axis=1, concat_axis=4, tiled=True)
    sectioned = lax.all_to_all(sectioned, "ctx", split_axis=0, concat_axis=3, tiled=True)
    return sectioned.reshape(local_blocks, ranks * lanes * positions, width)


def on_device(inputs, mixed, grad_out, left_weight, right_weight, first_weight, second_weight):
    ranks = lax.axis_size("ctx")
    lanes = lax.axis_size("chan")
    rows_here, tokens_here = inputs.shape
    local_blocks, bsize = (left_weight.shape[0], left_weight.shape[1])
    blocks_here = tokens_here // bsize
    width = rows_here * lanes
    groups, gsize = (first_weight.shape[0], first_weight.shape[1])
    got_x, got_y, got_g = (
        lax.all_to_all(
            inputs.reshape(rows_here, blocks_here, bsize),
            "chan",
            split_axis=1,
            concat_axis=0,
            tiled=True,
        ),
        lax.all_to_all(
            mixed.reshape(rows_here, blocks_here, bsize),
            "chan",
            split_axis=1,
            concat_axis=0,
            tiled=True,
        ),
        lax.all_to_all(
            grad_out.reshape(rows_here, blocks_here, bsize),
            "chan",
            split_axis=1,
            concat_axis=0,
            tiled=True,
        ),
    )
    block_x = jnp.transpose(got_x, (1, 2, 0))
    block_y = jnp.transpose(got_y, (1, 2, 0))
    block_g = jnp.transpose(got_g, (1, 2, 0))
    lower_left = lower_part(left_weight)
    inner = jnp.einsum(
        "ced,cdh->ceh", lower_left, block_x, preferred_element_type=jnp.float32
    ).astype(jnp.bfloat16)
    inner_cols = spread(inner, ranks, lanes)
    y_four = block_y.reshape(local_blocks, bsize, groups, gsize)
    g_four = block_g.reshape(local_blocks, bsize, groups, gsize).astype(jnp.float32)
    first_section = jnp.einsum(
        "ctgh,gkh->ctgk", y_four, first_weight, preferred_element_type=jnp.float32
    ).astype(jnp.bfloat16)
    gate_pre = jnp.einsum(
        "ctgk,kmg->ctmk", first_section, second_weight, preferred_element_type=jnp.float32
    )
    sig = jax.nn.sigmoid(gate_pre)
    y_float = y_four.astype(jnp.float32)
    gate_grad = (g_four * y_float * sig * (1.0 + gate_pre * (1.0 - sig))).astype(jnp.bfloat16)
    part_second = jnp.einsum(
        "ctmk,ctgk->kmg", gate_grad, first_section, preferred_element_type=jnp.float32
    )
    first_grad = jnp.einsum(
        "ctmk,kmg->ctgk", gate_grad, second_weight, preferred_element_type=jnp.float32
    ).astype(jnp.bfloat16)
    part_first = jnp.einsum(
        "ctgk,ctgh->gkh", first_grad, y_four, preferred_element_type=jnp.float32
    )
    back_term = jnp.einsum(
        "ctgk,gkh->ctgh", first_grad, first_weight, preferred_element_type=jnp.float32
    )
    mixed_grad = (
        (g_four * gate_pre * sig + back_term)
        .astype(jnp.bfloat16)
        .reshape(local_blocks, bsize, width)
    )
    grad_cols = spread(mixed_grad, ranks, lanes)
    lower_right = lower_part(right_weight)
    inner_grad_cols = jnp.einsum(
        "efc,feh->ceh", lower_right, grad_cols, preferred_element_type=jnp.float32
    ).astype(jnp.bfloat16)
    grad_right = lower_part(
        jnp.einsum("feh,ceh->efc", grad_cols, inner_cols, preferred_element_type=jnp.float32)
    ).astype(jnp.bfloat16)
    inner_grad = gather_back(inner_grad_cols, ranks, lanes)
    seq_term = jnp.einsum(
        "ced,ceh->cdh", lower_left, inner_grad, preferred_element_type=jnp.float32
    )
    result_blocks = (block_g.astype(jnp.float32) + seq_term).astype(jnp.bfloat16)
    grad_left = lower_part(
        jnp.einsum("ceh,cdh->ced", inner_grad, block_x, preferred_element_type=jnp.float32)
    ).astype(jnp.bfloat16)
    returned = lax.all_to_all(
        jnp.transpose(result_blocks, (2, 0, 1)), "chan", split_axis=0, concat_axis=1, tiled=True
    )
    grad_input = returned.reshape(rows_here, tokens_here)
    grad_first, grad_second = lax.psum((part_first, part_second), ("ctx", "chan"))
    return (grad_input, grad_left, grad_right, grad_first, grad_second)


def solution(mesh):
    in_specs = (
        P("chan", "ctx"),
        P("chan", "ctx"),
        P("chan", "ctx"),
        P(("ctx", "chan"), None, None),
        P(("ctx", "chan"), None, None),
        P(),
        P(),
    )
    out_specs = (
        P("chan", "ctx"),
        P(("ctx", "chan"), None, None),
        P(("ctx", "chan"), None, None),
        P(),
        P(),
    )
    return jax.shard_map(
        on_device, mesh=mesh, in_specs=in_specs, out_specs=out_specs, check_vma=False
    )
```

profile of v0, /device:TPU:1, one launch (start us, length us, event | category | flops | bytes accessed | tf_op | source)
XLA Modules:
  0.0 864.4 jit_solution(15877872118043095905)
XLA Ops:
  10.5 10.0 %all-to-all-start = ((bf16[64,32,512]{2,0,1:T(8,128)(2,1)}), bf16[64,32,512]{2,0,1:T(8,128)(2,1)S(1)}, u32[]{:S(2)}, u32[]{:S(2)}) async-start(bf16[64,32,512]{2,0,1:T(8,128)(2,1)} %bitcast.175), calls=%async_computation | async-start | bytes 4194304 | tf_op jit(solution)/shard_map/all_to_all | solution.py:54
  23.7 44.9 %all-to-all-done = bf16[64,32,512]{2,0,1:T(8,128)(2,1)S(1)} async-done(((bf16[64,32,512]{2,0,1:T(8,128)(2,1)}), bf16[64,32,512]{2,0,1:T(8,128)(2,1)S(1)}, u32[]{:S(2)}, u32[]{:S(2)}) %all-to-all-start) | async-done | bytes 2097184 | tf_op jit(solution)/shard_map/all_to_all | solution.py:54
  70.0 6.3 all-to-all-start.1
  81.4 5.5 copy.74
  86.9 5.4 copy.75
  92.3 32.1 %all-to-all-done.1 = bf16[64,32,512]{2,0,1:T(8,128)(2,1)S(1)} async-done(((bf16[64,32,512]{2,0,1:T(8,128)(2,1)}), bf16[64,32,512]{2,0,1:T(8,128)(2,1)S(1)}, u32[]{:S(2)}, u32[]{:S(2)}) %all-to-all-start.1) | async-done | bytes 2097184 | tf_op jit(solution)/shard_map/all_to_all | solution.py:47
  128.0 7.6 fusion.8
  139.8 8.2 fusion
  148.0 9.3 %copy.86 = bf16[1,512,32,64]{3,2,1,0:T(8,128)(2,1)} copy(bf16[1,512,32,64]{1,2,3,0:T(8,128)(2,1)} %fusion) | data formatting | bytes 4194304 | tf_op jit(solution)/shard_map/convert_element_type | solution.py:95
  157.3 7.6 reshape_reshape.3
  168.8 55.2 %all_to_all.150 = bf16[1,1,1,8,32,2,2048]{6,5,3,2,1,0,4:T(2,128)(2,1)S(1)} all-to-all(bf16[1,1,1,8,32,2,2048]{6,5,3,2,1,0,4:T(2,128)(2,1)S(1)} %copy.87), channel_id=1, replica_groups=mesh['ctx'=8,'chan'=32] {'chan'}, dimensions={4} | all-to-all | bytes 4194304 | tf_op jit(solution)/shard_map/all_to_all | solution.py:17
  227.1 8.1 all-to-all-start.3
  238.4 33.3 %all-to-all-done.3 = bf16[1,32,1,8,1,2,2048]{6,5,1,4,2,0,3:T(2,128)(2,1)} async-done(((bf16[1,32,1,8,1,2,2048]{6,5,1,4,2,0,3:T(2,128)(2,1)}), bf16[1,32,1,8,1,2,2048]{6,5,1,4,2,0,3:T(2,128)(2,1)}, u32[]{:S(2)}, u32[]{:S(2)}) %all-to-all-start.3) | async-done | bytes 2097184 | tf_op jit(solution)/shard_map/all_to_all | solution.py:18
  271.7 21.2 %all-to-all-start.7 = ((bf16[64,32,512]{2,0,1:T(8,128)(2,1)}), bf16[64,32,512]{2,0,1:T(8,128)(2,1)}, u32[]{:S(2)}, u32[]{:S(2)}) async-start(bf16[64,32,512]{2,0,1:T(8,128)(2,1)} %bitcast.174), calls=%async_computation.7 | async-start | bytes 4194304 | tf_op jit(solution)/shard_map/all_to_all | solution.py:40
  300.3 40.7 %all-to-all-done.7 = bf16[64,32,512]{2,0,1:T(8,128)(2,1)} async-done(((bf16[64,32,512]{2,0,1:T(8,128)(2,1)}), bf16[64,32,512]{2,0,1:T(8,128)(2,1)}, u32[]{:S(2)}, u32[]{:S(2)}) %all-to-all-start.7) | async-done | bytes 2097184 | tf_op jit(solution)/shard_map/all_to_all | solution.py:40
  341.1 6.8 all-to-all-start.4
  361.7 34.1 %all-to-all-done.4 = bf16[8,32,1,1,1,2,2048]{6,5,0,4,3,2,1:T(2,128)(2,1)} async-done(((bf16[8,32,1,1,1,2,2048]{6,5,0,4,3,2,1:T(2,128)(2,1)}), bf16[8,32,1,1,1,2,2048]{6,5,0,4,3,2,1:T(2,128)(2,1)}, u32[]{:S(2)}, u32[]{:S(2)}) %all-to-all-start.4) | async-done | bytes 2097184 | tf_op jit(solution)/shard_map/all_to_all | solution.py:26
  395.8 6.4 all-to-all-start.8
  406.9 43.5 %all-to-all-done.8 = bf16[1,1,1,8,32,2,2048]{6,5,3,2,1,0,4:T(2,128)(2,1)} async-done(((bf16[1,1,1,8,32,2,2048]{6,5,3,2,1,0,4:T(2,128)(2,1)}), bf16[1,1,1,8,32,2,2048]{6,5,3,2,1,0,4:T(2,128)(2,1)}, u32[]{:S(2)}, u32[]{:S(2)}) %all-to-all-start.8) | async-done | bytes 2097184 | tf_op jit(solution)/shard_map/all_to_all | solution.py:17
  459.5 29.0 %all-to-all-done.5 = bf16[8,1,1,1,32,2,2048]{6,5,4,3,2,1,0:T(2,128)(2,1)} async-done(((bf16[8,1,1,1,32,2,2048]{6,5,4,3,2,1,0:T(2,128)(2,1)}), bf16[8,1,1,1,32,2,2048]{6,5,4,3,2,1,0:T(2,128)(2,1)}, u32[]{:S(2)}, u32[]{:S(2)}) %all-to-all-start.5) | async-done | bytes 2097184 | tf_op jit(solution)/shard_map/all_to_all | solution.py:27
  515.9 11.7 %all-to-all-done.9 = bf16[1,32,1,8,1,2,2048]{6,5,1,4,2,0,3:T(2,128)(2,1)} async-done(((bf16[1,32,1,8,1,2,2048]{6,5,1,4,2,0,3:T(2,128)(2,1)}), bf16[1,32,1,8,1,2,2048]{6,5,1,4,2,0,3:T(2,128)(2,1)}, u32[]{:S(2)}, u32[]{:S(2)}) %all-to-all-start.9) | async-done | bytes 2097184 | tf_op jit(solution)/shard_map/all_to_all | solution.py:18
  527.6 32.9 %all-to-all-start.6 = ((bf16[32,2,16384]{2,1,0:T(2,128)(2,1)}), bf16[32,2,16384]{2,1,0:T(2,128)(2,1)}, u32[]{:S(2)}, u32[]{:S(2)}) async-start(bf16[32,2,16384]{2,1,0:T(2,128)(2,1)} %reshape.164), calls=%async_computation.6 | async-start | bytes 4194304 | tf_op jit(solution)/shard_map/all_to_all | solution.py:114
  567.9 263.2 %all-reduce.3.cloned.1.call-done = (f32[32,64,64]{2,1,0:T(8,128)}, f32[64,32,32]{2,1,0:T(8,128)}) async-done(((f32[32,64,64]{2,1,0:T(8,128)}, f32[64,32,32]{2,1,0:T(8,128)}), (f32[32,64,64]{2,1,0:T(8,128)}, f32[64,32,32]{2,1,0:T(8,128)})) %all-reduce.3.cloned.1.call-update) | async-done | bytes 786448 | tf_op jit(solution)/shard_map/psum | solution.py:118
  841.5 10.5 %reshape.165 = bf16[2048,1,512]{2,1,0:T(2,128)(2,1)} reshape(bf16[32,2,16384]{2,1,0:T(2,128)(2,1)} %all-to-all-done.6) | data formatting | bytes 4194304
  (70 shorter events, 116.1 us)
Async XLA Ops:
  7.2 117.9 %copy-start = (bf16[32,64,64]{2,1,0:T(8,128)(2,1)S(1)}, bf16[32,64,64]{2,1,0:T(8,128)(2,1)}, u32[]{:S(2)}) copy-start(bf16[32,64,64]{2,1,0:T(8,128)(2,1)} %param.12) | copy-start | bytes 786436
  10.5 58.2 %all-to-all-start = ((bf16[64,32,512]{2,0,1:T(8,128)(2,1)}), bf16[64,32,512]{2,0,1:T(8,128)(2,1)S(1)}, u32[]{:S(2)}, u32[]{:S(2)}) async-start(bf16[64,32,512]{2,0,1:T(8,128)(2,1)} %bitcast.175), calls=%async_computation | async-start | bytes 4194304 | tf_op jit(solution)/shard_map/all_to_all | solution.py:54
  68.6 1.4 copy-start.5
  68.6 7.7 copy-start.13
  70.0 54.5 %all-to-all-start.1 = ((bf16[64,32,512]{2,0,1:T(8,128)(2,1)}), bf16[64,32,512]{2,0,1:T(8,128)(2,1)S(1)}, u32[]{:S(2)}, u32[]{:S(2)}) async-start(bf16[64,32,512]{2,0,1:T(8,128)(2,1)} %bitcast.173), calls=%async_computation.1 | async-start | bytes 4194304 | tf_op jit(solution)/shard_map/all_to_all | solution.py:47
  125.1 2.9 copy-start.4
  125.8 9.8 %copy-start.6 = (bf16[512,32,64]{0,2,1:T(8,128)(2,1)}, bf16[512,32,64]{0,2,1:T(8,128)(2,1)S(1)}, u32[]{:S(2)}) copy-start(bf16[512,32,64]{0,2,1:T(8,128)(2,1)S(1)} %convert_bitcast_fusion.1) | copy-start | bytes 6291460
  136.9 2.9 copy-start.2
  227.1 44.6 %all-to-all-start.3 = ((bf16[1,32,1,8,1,2,2048]{6,5,1,4,2,0,3:T(2,128)(2,1)}), bf16[1,32,1,8,1,2,2048]{6,5,1,4,2,0,3:T(2,128)(2,1)}, u32[]{:S(2)}, u32[]{:S(2)}) async-start(bf16[1,32,1,8,1,2,2048]{6,5,1,4,2,0,3:T(2,128)(2,1)} %copy.88), calls=%async_computation.3 | async-start | bytes 4194304 | tf_op jit(solution)/shard_map/all_to_all | solution.py:18
  271.7 69.4 %all-to-all-start.7 = ((bf16[64,32,512]{2,0,1:T(8,128)(2,1)}), bf16[64,32,512]{2,0,1:T(8,128)(2,1)}, u32[]{:S(2)}, u32[]{:S(2)}) async-start(bf16[64,32,512]{2,0,1:T(8,128)(2,1)} %bitcast.174), calls=%async_computation.7 | async-start | bytes 4194304 | tf_op jit(solution)/shard_map/all_to_all | solution.py:40
  292.9 2.5 copy-start.14
  295.4 1.4 copy-start.8
  300.3 47.5 %copy-start.11 = (bf16[1,512,512]{2,1,0:T(8,128)(2,1)S(1)}, bf16[1,512,512]{2,1,0:T(8,128)(2,1)}, u32[]{:S(2)}) copy-start(bf16[1,512,512]{2,1,0:T(8,128)(2,1)} %param.10) | copy-start | bytes 1572868
  341.1 54.8 %all-to-all-start.4 = ((bf16[8,32,1,1,1,2,2048]{6,5,0,4,3,2,1:T(2,128)(2,1)}), bf16[8,32,1,1,1,2,2048]{6,5,0,4,3,2,1:T(2,128)(2,1)}, u32[]{:S(2)}, u32[]{:S(2)}) async-start(bf16[8,32,1,1,1,2,2048]{6,5,0,4,3,2,1:T(2,128)(2,1)} %copy.91), calls=%async_computation.4 | async-start | bytes 4194304 | tf_op jit(solution)/shard_map/all_to_all | solution.py:26
  395.8 54.6 %all-to-all-start.8 = ((bf16[1,1,1,8,32,2,2048]{6,5,3,2,1,0,4:T(2,128)(2,1)}), bf16[1,1,1,8,32,2,2048]{6,5,3,2,1,0,4:T(2,128)(2,1)}, u32[]{:S(2)}, u32[]{:S(2)}) async-start(bf16[1,1,1,8,32,2,2048]{6,5,3,2,1,0,4:T(2,128)(2,1)} %copy.97), calls=%async_computation.8 | async-start | bytes 4194304 | tf_op jit(solution)/shard_map/all_to_all | solution.py:17
  450.4 38.1 %all-to-all-start.5 = ((bf16[8,1,1,1,32,2,2048]{6,5,4,3,2,1,0:T(2,128)(2,1)}), bf16[8,1,1,1,32,2,2048]{6,5,4,3,2,1,0:T(2,128)(2,1)}, u32[]{:S(2)}, u32[]{:S(2)}) async-start(bf16[8,1,1,1,32,2,2048]{6,5,4,3,2,1,0:T(2,128)(2,1)} %copy.92), calls=%async_computation.5 | async-start | bytes 4194304 | tf_op jit(solution)/shard_map/all_to_all | solution.py:27
  488.5 39.1 %all-to-all-start.9 = ((bf16[1,32,1,8,1,2,2048]{6,5,1,4,2,0,3:T(2,128)(2,1)}), bf16[1,32,1,8,1,2,2048]{6,5,1,4,2,0,3:T(2,128)(2,1)}, u32[]{:S(2)}, u32[]{:S(2)}) async-start(bf16[1,32,1,8,1,2,2048]{6,5,1,4,2,0,3:T(2,128)(2,1)} %copy.98), calls=%async_computation.9 | async-start | bytes 4194304 | tf_op jit(solution)/shard_map/all_to_all | solution.py:18
  527.6 314.0 %all-to-all-start.6 = ((bf16[32,2,16384]{2,1,0:T(2,128)(2,1)}), bf16[32,2,16384]{2,1,0:T(2,128)(2,1)}, u32[]{:S(2)}, u32[]{:S(2)}) async-start(bf16[32,2,16384]{2,1,0:T(2,128)(2,1)} %reshape.164), calls=%async_computation.6 | async-start | bytes 4194304 | tf_op jit(solution)/shard_map/all_to_all | solution.py:114
  560.5 270.6 %all-reduce.3.cloned.1.call-start = ((), (), s32[]{:S(2)}) async-start(), calls=%async_computation.10 | async-start | bytes 4194304 | tf_op jit(solution)/shard_map/psum | solution.py:118
  560.8 4.8 copy-start.3
  833.7 2.6 copy-start.9
  836.3 1.6 copy-start.10
  854.8 1.5 copy-start.12
  854.8 2.5 copy-start.1
  (1 other events, 1.3 us)
Sparse Core Ops, SparseCore 0:
  568.1 263.0 all-reduce.2
where the time goes:
time: 876 us; the launch traced here: 864 us
  waiting for transfers between devices  533 us (61%)
  local copies, waits for them, and re-layouts  109 us (12%)
  starting transfers between devices  101 us (12%)
  blocking collectives  55.2 us (6%)
  matrix products  34.5 us (4%)
  other arithmetic  17.6 us (2%)
  between operations  14.5 us (2%)
    psum x1, waiting for transfers between devices, on_device(): lax.psum((part_first, part_second), ('ctx', 'chan'))  263 us
    all_to_all x1, blocking collectives, spread(): lax.all_to_all(sectioned, 'chan', split_axis=4, concat_axis=1, tiled=True)  55.2 us
    all_to_all x2, waiting for transfers between devices, spread(): lax.all_to_all(sectioned, 'ctx', split_axis=3, concat_axis=0, tiled=True)  45 us
    all_to_all x1, waiting for transfers between devices, on_device(): lax.all_to_all(grad_out.reshape(rows_here, blocks_here, bsize), 'chan', s...  44.9 us
    all_to_all x1, waiting for transfers between devices, spread(): lax.all_to_all(sectioned, 'chan', split_axis=4, concat_axis=1, tiled=True)  43.5 us
    all_to_all x1, waiting for transfers between devices, on_device(): lax.all_to_all(inputs.reshape(rows_here, blocks_here, bsize), 'chan', spl...  40.7 us
    all_to_all x1, waiting for transfers between devices, gather_back(): lax.all_to_all(sectioned, 'chan', split_axis=1, concat_axis=4, tiled=True)  34.1 us
    all_to_all x1, starting transfers between devices, on_device(): lax.all_to_all(jnp.transpose(result_blocks, (2, 0, 1)), 'chan', split_axi...  32.9 us
  transfers between devices with their start and end apart: 10, of which 9 were waited for; matrix products, arithmetic and copies ran while one was open for 11% of the time, Pallas kernels for 0%

commit v1 on v0

v1 whole, which is shorter than its diff:
```python
import functools

import jax
import jax.numpy as jnp
from jax import lax
from jax.experimental import pallas as pl
from jax.experimental.pallas import tpu as pltpu
from jax.sharding import PartitionSpec as P

MESH = pl.DeviceIdType.MESH
ANY = pl.BlockSpec(memory_space=pl.ANY)
NCTX, NCHAN, NDEV, HALF = 8, 32, 256, 16
BS, CB, CG, NB, D = 512, 64, 32, 256, 2048
KC = 16
F32, BF16 = jnp.float32, jnp.bfloat16


def coords():
    return lax.axis_index("ctx"), lax.axis_index("chan")


def chan_dev(chan):
    return (lax.axis_index("ctx"), chan)


def any_dev(linear):
    return (linear // NCHAN, lax.rem(linear, NCHAN))


def al(value, size):
    return pl.multiple_of(value * size, size)


def enter(count, device_of):
    barrier = pltpu.get_barrier_semaphore()

    @pl.loop(1, count)
    def _(step):
        pl.semaphore_signal(barrier, inc=1, device_id=device_of(step), device_id_type=MESH)

    pl.semaphore_wait(barrier, count - 1)


def remote(src, dst, send, recv, device):
    return pltpu.make_async_remote_copy(
        src_ref=src, dst_ref=dst, send_sem=send, recv_sem=recv, device_id=device, device_id_type=MESH
    )


def collect_kernel(
    x_ref, y_ref, g_ref, left_ref, xp_ref, yt_ref, gt_ref, lp_ref, send, recv, local
):
    ctx, me = coords()
    half, slot = me // HALF, lax.rem(me, HALF)
    partner = lax.rem(me + HALF, NCHAN)
    enter(NCHAN, lambda step: chan_dev(lax.rem(me + step, NCHAN)))

    def whole(src, dst, index, peer):
        return remote(
            src.at[:, pl.ds(al(peer, BS), BS)],
            dst.at[pl.ds(al(me, CB), CB), :],
            send.at[index],
            recv.at[index],
            chan_dev(peer),
        )

    def paired(part, other):
        return remote(
            x_ref.at[:, pl.ds(al(other + HALF * part, BS), BS)],
            xp_ref.at[part, pl.ds(al(slot, CB), CB), :],
            send.at[part],
            recv.at[part],
            chan_dev(half * HALF + other),
        )

    locals_ = [
        pltpu.make_async_copy(left_ref.at[0], lp_ref.at[half], local.at[0]),
        pltpu.make_async_copy(
            y_ref.at[:, pl.ds(al(me, BS), BS)], yt_ref.at[pl.ds(al(me, CB), CB), :], local.at[1]
        ),
        pltpu.make_async_copy(
            g_ref.at[:, pl.ds(al(me, BS), BS)], gt_ref.at[pl.ds(al(me, CB), CB), :], local.at[2]
        ),
    ]
    for part in range(2):
        locals_.append(
            pltpu.make_async_copy(
                x_ref.at[:, pl.ds(al(slot + HALF * part, BS), BS)],
                xp_ref.at[part, pl.ds(al(slot, CB), CB), :],
                local.at[3 + part],
            )
        )
    for copy in locals_:
        copy.start()
    left_copy = remote(left_ref.at[0], lp_ref.at[half], send.at[4], recv.at[4], chan_dev(partner))
    left_copy.start()

    @pl.loop(1, NCHAN)
    def _(step):
        whole(y_ref, yt_ref, 2, lax.rem(me + step, NCHAN)).start()

    @pl.loop(1, HALF)
    def _(step):
        other = lax.rem(slot + step, HALF)
        paired(0, other).start()
        paired(1, other).start()

    @pl.loop(1, NCHAN)
    def _(step):
        whole(g_ref, gt_ref, 3, lax.rem(me + step, NCHAN)).start()

    for copy in locals_:
        copy.wait()
    left_copy.wait()
    for part in range(2):
        area = xp_ref.at[part, pl.ds(0, (HALF - 1) * CB), :]
        remote(area, area, send.at[part], recv.at[part], chan_dev(partner)).wait()
    for index, dst in ((2, yt_ref), (3, gt_ref)):
        area = dst.at[pl.ds(0, (NCHAN - 1) * CB), :]
        remote(area, area, send.at[index], recv.at[index], chan_dev(partner)).wait()


def collect(x, y, g, left):
    return pl.pallas_call(
        collect_kernel,
        out_shape=[
            jax.ShapeDtypeStruct((2, HALF * CB, BS), BF16),
            jax.ShapeDtypeStruct((D, BS), BF16),
            jax.ShapeDtypeStruct((D, BS), BF16),
            jax.ShapeDtypeStruct((2, BS, BS), BF16),
        ],
        in_specs=[ANY] * 4,
        out_specs=[ANY] * 4,
        scratch_shapes=[
            pltpu.SemaphoreType.DMA((5,)),
            pltpu.SemaphoreType.DMA((5,)),
            pltpu.SemaphoreType.DMA((5,)),
        ],
        compiler_params=pltpu.CompilerParams(collective_id=1, has_side_effects=True),
        name="collect",
    )(x, y, g, left)


def linear_me():
    ctx, chan = coords()
    return ctx * NCHAN + chan


def plane_peer(step):
    ctx, chan = coords()
    y, z_hi, z_lo, xc = ctx // 2, lax.rem(ctx, 2), chan // 8, lax.rem(chan, 8)
    here = y * 8 + xc
    peer = lax.rem(here + step, 32)
    return here, peer, ((peer // 8) * 2 + z_hi, z_lo * 8 + lax.rem(peer, 8))


def column_peer(step):
    ctx, chan = coords()
    y, z_hi, z_lo, xc = ctx // 2, lax.rem(ctx, 2), chan // 8, lax.rem(chan, 8)
    here = z_hi * 4 + z_lo
    peer = lax.rem(here + step, 8)
    return here, peer, (y * 2 + peer // 4, lax.rem(peer, 4) * 8 + xc)


def everywhere(step):
    me = linear_me()
    peer = lax.rem(me + step, NDEV)
    return me, peer, any_dev(peer)


def exchange_kernel(groups, *refs):
    count = len(groups)
    srcs, dsts = refs[:count], refs[count : 2 * count]
    send, recv, local = refs[2 * count :]
    enter(NDEV, lambda step: everywhere(step)[2])

    def copy_of(index, step):
        here, peer, device = groups[index][1](step)
        return remote(
            srcs[index].at[peer], dsts[index].at[here], send.at[index], recv.at[index], device
        )

    locals_ = []
    for index, (_, peers) in enumerate(groups):
        here = peers(0)[0]
        locals_.append(
            pltpu.make_async_copy(srcs[index].at[here], dsts[index].at[here], local.at[index])
        )
    for copy in locals_:
        copy.start()
    for index, (size, _) in enumerate(groups):

        @pl.loop(1, size)
        def _(step, index=index):
            copy_of(index, step).start()

    for copy in locals_:
        copy.wait()
    for index, (size, peers) in enumerate(groups):
        area = dsts[index].at[pl.ds(0, size - 1)]
        remote(area, area, send.at[index], recv.at[index], peers(1)[2]).wait()


def exchange(arrays, groups, collective_id):
    count = len(arrays)
    return pl.pallas_call(
        functools.partial(exchange_kernel, groups),
        out_shape=[jax.ShapeDtypeStruct(a.shape, a.dtype) for a in arrays],
        in_specs=[ANY] * count,
        out_specs=[ANY] * count,
        scratch_shapes=[
            pltpu.SemaphoreType.DMA((count,)),
            pltpu.SemaphoreType.DMA((count,)),
            pltpu.SemaphoreType.DMA((count,)),
        ],
        compiler_params=pltpu.CompilerParams(collective_id=collective_id, has_side_effects=True),
        name="exchange",
    )(*arrays)


def give_back_kernel(ret_ref, grad_ref, term_ref, out_ref, got_ref, all_ref, send, recv, local):
    ctx, me = coords()
    half, slot = me // HALF, lax.rem(me, HALF)
    partner = lax.rem(me + HALF, NCHAN)
    here, _, _ = plane_peer(0)
    level, _, _ = column_peer(0)
    owned = here * 8 + level
    enter(NDEV, lambda step: everywhere(step)[2])

    def paired(part, other):
        return remote(
            ret_ref.at[part, pl.ds(al(other, CB), CB), :],
            out_ref.at[:, pl.ds(al(slot + HALF * part, BS), BS)],
            send.at[part],
            recv.at[part],
            chan_dev(half * HALF + other),
        )

    def shared(step):
        return remote(
            term_ref, all_ref.at[owned], send.at[3], recv.at[3], everywhere(step)[2]
        )

    locals_ = [pltpu.make_async_copy(term_ref, all_ref.at[owned], local.at[2])]
    for part in range(2):
        locals_.append(
            pltpu.make_async_copy(
                ret_ref.at[part, pl.ds(al(slot, CB), CB), :],
                out_ref.at[:, pl.ds(al(slot + HALF * part, BS), BS)],
                local.at[part],
            )
        )
    for copy in locals_:
        copy.start()
    grad_copy = remote(
        grad_ref.at[1 - half], got_ref, send.at[2], recv.at[2], chan_dev(partner)
    )
    grad_copy.start()

    @pl.loop(1, HALF)
    def _(step):
        other = lax.rem(slot + step, HALF)
        paired(0, other).start()
        paired(1, other).start()

    @pl.loop(1, NDEV)
    def _(step):
        shared(step).start()

    for copy in locals_:
        copy.wait()
    grad_copy.wait()
    for part in range(2):
        area = ret_ref.at[part, pl.ds(0, (HALF - 1) * CB), :]
        remote(area, area, send.at[part], recv.at[part], chan_dev(partner)).wait()
    area = all_ref.at[pl.ds(0, NDEV - 1)]
    remote(area, area, send.at[3], recv.at[3], chan_dev(partner)).wait()


def give_back(ret, grad, term):
    return pl.pallas_call(
        give_back_kernel,
        out_shape=[
            jax.ShapeDtypeStruct((CB, NCHAN * BS), BF16),
            jax.ShapeDtypeStruct((BS, BS), BF16),
            jax.ShapeDtypeStruct((NDEV, 8, 128), F32),
        ],
        in_specs=[ANY] * 3,
        out_specs=[ANY] * 3,
        scratch_shapes=[
            pltpu.SemaphoreType.DMA((4,)),
            pltpu.SemaphoreType.DMA((4,)),
            pltpu.SemaphoreType.DMA((3,)),
        ],
        compiler_params=pltpu.CompilerParams(collective_id=4, has_side_effects=True),
        name="give_back",
    )(ret, grad, term)


def dot(a, b, dims):
    return lax.dot_general(a, b, (dims, ((), ())), preferred_element_type=F32)


NN, NT, TN = ((1,), (0,)), ((1,), (1,)), ((0,), (0,))


def channel_kernel(
    y_ref, g_ref, w_ref, s_ref, eye_ref, pick_ref, mg_ref, pf_ref, ps_ref, fs, fg, gated
):
    for q in range(8):
        rows = pl.ds(q * 4, 4)
        fs[rows] = dot(w_ref[q], y_ref[rows].reshape(256, BS), NN).astype(BF16).reshape(4, CB, BS)
    for i in range(CB // KC):
        cols = pl.ds(i * KC, KC)
        s = s_ref[i]
        section = fs[:, cols, :].reshape(CG * KC, BS)
        pre = dot(s, section, NN)
        y = y_ref[:, cols, :].reshape(CG * KC, BS).astype(F32)
        g = g_ref[:, cols, :].reshape(CG * KC, BS).astype(F32)
        sig = jax.nn.sigmoid(pre)
        gsig = g * sig
        gg = (gsig * y * (1.0 + pre * (1.0 - sig))).astype(BF16)
        gated[:, cols, :] = (gsig * pre).reshape(CG, KC, BS)
        fg[:, cols, :] = dot(s, gg, TN).astype(BF16).reshape(CG, KC, BS)
        both = dot(gg, section, NT)
        row = lax.broadcasted_iota(jnp.int32, both.shape, 0)
        col = lax.broadcasted_iota(jnp.int32, both.shape, 1)
        both = jnp.where(lax.rem(row, KC) == lax.rem(col, KC), both, 0.0)
        ps_ref[i] = lax.dot_general(
            both,
            pick_ref[...],
            (NN, ((), ())),
            preferred_element_type=F32,
            precision=lax.Precision.HIGHEST,
        )
    for q in range(8):
        rows = pl.ds(q * 4, 4)
        fgq = fg[rows].reshape(256, BS)
        back = dot(w_ref[q], fgq, TN)
        mg = (gated[rows].reshape(256, BS) + back).astype(BF16)
        mg_ref[:, pl.ds(q * 256, 256)] = dot(eye_ref[...], mg, NT).astype(BF16)
        pf = dot(fgq, y_ref[rows].reshape(256, BS), NT)
        for a in range(4):
            pf_ref[q * 4 + a] = pf[a * CB : (a + 1) * CB, a * CB : (a + 1) * CB]


def channel(y, g, w, s, eye, pick):
    vmem = pl.BlockSpec(memory_space=pltpu.VMEM)
    return pl.pallas_call(
        channel_kernel,
        out_shape=[
            jax.ShapeDtypeStruct((BS, D), BF16),
            jax.ShapeDtypeStruct((CG, CB, CB), F32),
            jax.ShapeDtypeStruct((CB // KC, CG * KC, CG), F32),
        ],
        in_specs=[vmem] * 6,
        out_specs=[vmem] * 3,
        scratch_shapes=[
            pltpu.VMEM((CG, CB, BS), BF16),
            pltpu.VMEM((CG, CB, BS), BF16),
            pltpu.VMEM((CG, CB, BS), F32),
        ],
        compiler_params=pltpu.CompilerParams(vmem_limit_bytes=48 * 1024 * 1024),
        name="channel",
    )(y.reshape(CG, CB, BS), g.reshape(CG, CB, BS), w, s, eye, pick)


def lower_part(weight):
    size = weight.shape[-1]
    rows = lax.broadcasted_iota(jnp.int32, (size, size), 0)
    cols = lax.broadcasted_iota(jnp.int32, (size, size), 1)
    return jnp.where(rows >= cols, weight, jnp.zeros_like(weight))


def ein(spec, a, b):
    return jnp.einsum(spec, a, b, preferred_element_type=F32)


def on_device(inputs, mixed, grad_out, left_weight, right_weight, first_weight, second_weight):
    half = lax.axis_index("chan") // HALF
    eye4, eye16 = jnp.eye(4, dtype=BF16), jnp.eye(KC, dtype=BF16)
    w = (
        first_weight.reshape(8, 4, CB, 1, CB) * eye4[None, :, None, :, None]
    ).reshape(8, 4 * CB, 4 * CB)
    s = (
        second_weight.reshape(CB // KC, KC, CG, CG).transpose(0, 2, 1, 3)[..., None]
        * eye16[None, None, :, None, :]
    ).reshape(CB // KC, CG * KC, CG * KC)
    eye = jnp.eye(BS, dtype=BF16)
    pick = jnp.repeat(jnp.eye(CG, dtype=F32), KC, axis=0)

    xp, yt, gt, lp = collect(inputs, mixed, grad_out, left_weight)
    lower_left = lower_part(lp)
    mg, part_first, part_second = channel(yt, gt, w, s, eye, pick)
    inner = ein("sed,shd->seh", lower_left, xp).astype(BF16)
    inner_out = inner.reshape(2, NDEV, 2, HALF * CB).transpose(1, 0, 2, 3)
    part_second = part_second.reshape(CB // KC, CG, KC, CG).transpose(0, 2, 1, 3)
    parts = jnp.concatenate(
        [part_first.reshape(-1), part_second.reshape(-1), jnp.zeros((CB * CG * CG,), F32)]
    ).reshape(32, 8, 8, 128)
    mg_cols, inner_cols, parts = exchange(
        [mg.reshape(NDEV, 2, D), inner_out, parts],
        ((NDEV, everywhere), (NDEV, everywhere), (32, plane_peer)),
        2,
    )
    parts = jnp.sum(parts, axis=0)
    lower_right = lower_part(right_weight)
    inner_grad = ein("efc,feh->ceh", lower_right, mg_cols).astype(BF16)
    inner_cols = inner_cols.reshape(NCTX, 2, HALF, 2, 2, HALF * CB)
    inner_cols = inner_cols.transpose(4, 0, 3, 2, 1, 5).reshape(2, NB, D)
    grad_back = inner_grad.reshape(NCTX, 2, HALF, 2, 2, HALF * CB).transpose(0, 4, 2, 1, 3, 5)
    grad_back, parts = exchange(
        [grad_back.reshape(NDEV, 2, 2, HALF * CB), parts],
        ((NDEV, everywhere), (8, column_peer)),
        3,
    )
    grad_right = lower_part(ein("feh,ech->efc", mg_cols, inner_cols)).astype(BF16)
    parts = jnp.sum(parts, axis=0)
    grad_back = grad_back.transpose(1, 0, 2, 3).reshape(2, BS, HALF * CB)
    seq_term = ein("sed,seh->shd", lower_left, grad_back).astype(BF16)
    grad_left = ein("seh,shd->sed", grad_back, xp)
    seq_term, grad_other, parts = give_back(seq_term, grad_left.astype(BF16), parts)
    grad_input = (grad_out.astype(F32) + seq_term.astype(F32)).astype(BF16)
    own = lax.dynamic_index_in_dim(grad_left, half, 0, keepdims=False)
    grad_left = lower_part(own + grad_other.astype(F32)).astype(BF16)[None]
    parts = parts.reshape(-1)
    grad_first = parts[: CG * CB * CB].reshape(CG, CB, CB)
    grad_second = parts[CG * CB * CB : CG * CB * CB + CB * CG * CG].reshape(CB, CG, CG)
    return (grad_input, grad_left, grad_right, grad_first, grad_second)


def solution(mesh):
    in_specs = (
        P("chan", "ctx"),
        P("chan", "ctx"),
        P("chan", "ctx"),
        P(("ctx", "chan"), None, None),
        P(("ctx", "chan"), None, None),
        P(),
        P(),
    )
    out_specs = (
        P("chan", "ctx"),
        P(("ctx", "chan"), None, None),
        P(("ctx", "chan"), None, None),
        P(),
        P(),
    )
    return jax.shard_map(
        on_device, mesh=mesh, in_specs=in_specs, out_specs=out_specs, check_vma=False
    )
```

time: 876 us -> 519 us (0.59)
  waiting for transfers between devices: 533 us -> 0 us
  Pallas kernels: 0 us -> 396 us
  starting transfers between devices: 101 us -> 0 us
  blocking collectives: 55.2 us -> 0 us
  local copies, waits for them, and re-layouts: 109 us -> 89.6 us
  matrix products: 34.5 us -> 16.6 us
  between operations: 14.5 us -> 1.17 us
    pallas_call x0 -> x5, Pallas kernels: none -> 396 us  [the longest x2 177 us: exchange(): pl.pallas_call(functools.partial(exchange_kernel, groups), out_shape=[jax...]
    all_to_all x9 -> x0, waiting for transfers between devices: 270 us -> none  [the longest x2 45 us: spread(): lax.all_to_all(sectioned, 'ctx', split_axis=3, concat_axis=0, tiled=True)]
    psum x1 -> x0, waiting for transfers between devices: 263 us -> none  [on_device(): lax.psum((part_first, part_second), ('ctx', 'chan'))]
    all_to_all x9 -> x0, starting transfers between devices: 100 us -> none  [the longest x1 32.9 us: on_device(): lax.all_to_all(jnp.transpose(result_blocks, (2, 0, 1)), 'chan', split_axi...]
    all_to_all x1 -> x0, blocking collectives: 55.2 us -> none  [spread(): lax.all_to_all(sectioned, 'chan', split_axis=4, concat_axis=1, tiled=True)]
    mul x0 -> x8, local copies, waits for them, and re-layouts: none -> 52.6 us  [the longest x4 49.7 us: on_device(): second_weight.reshape(CB // KC, KC, CG, CG).transpose(0, 2, 1, 3)[..., None]]
    unnamed x38 -> x23, local copies, waits for them, and re-layouts: 32.6 us -> 0.82 us
    dot_general x11 -> x5, matrix products: 34.5 us -> 16.6 us  [ein(): return jnp.einsum(spec, a, b, preferred_element_type=F32)]
  transfers between devices with their start and end apart: 10 -> 0, of which waited for: 9 -> 0; matrix products, arithmetic and copies ran while one was open for 11% -> 0% of each run, Pallas kernels for 0% -> 0%
where the time goes in v1:
time: 519 us; the launch traced here: 513 us
  Pallas kernels  396 us (76%)
  local copies, waits for them, and re-layouts  89.6 us (17%)
  matrix products  16.6 us (3%)
  other arithmetic  9.53 us (2%)
    pallas_call x2, Pallas kernels, exchange(): pl.pallas_call(functools.partial(exchange_kernel, groups), out_shape=[jax...  177 us
    pallas_call x1, Pallas kernels, collect(): pl.pallas_call(collect_kernel, out_shape=[jax.ShapeDtypeStruct((2, HALF *...  124 us
    pallas_call x1, Pallas kernels, give_back(): pl.pallas_call(give_back_kernel, out_shape=[jax.ShapeDtypeStruct((CB, NCH...  81.9 us
    mul x4, local copies, waits for them, and re-layouts, on_device(): second_weight.reshape(CB // KC, KC, CG, CG).transpose(0, 2, 1, 3)[..., None]  49.7 us
    dot_general x5, matrix products, ein(): return jnp.einsum(spec, a, b, preferred_element_type=F32)  16.6 us
    pallas_call x1, Pallas kernels, channel(): pl.pallas_call(channel_kernel, out_shape=[jax.ShapeDtypeStruct((BS, D), B...  13.1 us

profile of v1, /device:TPU:1, one launch (start us, length us, event | category | flops | bytes accessed | tf_op | source)
XLA Modules:
  0.0 512.9 jit_solution(11382544710132621984)
XLA Ops:
  0.6 124.3 %collect.1 = (bf16[2,1024,512]{2,1,0:T(8,128)(2,1)}, bf16[2048,512]{1,0:T(8,128)(2,1)}, bf16[2048,512]{1,0:T(8,128)(2,1)}, bf16[2,512,512]{2,1,0:T(8,128)(2,1)}) custom-call(bf16[64,16384]{1,0:T(8,128)(2,1)} %x_ref.1, bf16[64,16384]{1,0:T(8,128)(2,1)} %y_ref.1, bf16[64,16384]{1,0:T(8,128)(2,1)} %g_ref.1, bf16[1,512,512]{2,1,0:T(8,128)(2,1)} %left_ref.1), custom_call_target="tpu_custom_call" | custom-call | tf_op jit(solution)/shard_map/collect/pallas_call | solution.py:124
  126.0 11.0 %mul.49 = bf16[4,32,16,32,16]{4,3,2,1,0:T(8,128)(2,1)} broadcast(bf16[4,32,16,32]{3,2,1,0:T(8,128)(2,1)S(1)} %copy.20), dimensions={0,1,2,3} | broadcast | bytes 2228224 | tf_op jit(solution)/shard_map/mul | solution.py:386
  137.0 27.9 %mul.50 = bf16[4,512,512]{2,1,0:T(8,128)(2,1)S(1)} reshape(bf16[4,32,16,32,16]{4,3,2,1,0:T(8,128)(2,1)} %mul.49) | data formatting | bytes 4194304 | tf_op jit(solution)/shard_map/mul | solution.py:386
  165.0 2.9 mul.51
  167.9 7.8 %mul.52 = bf16[512,512]{1,0:T(8,128)(2,1)S(1)} reshape(bf16[32,16,32,16]{3,2,1,0:T(8,128)(2,1)} %mul.51) | data formatting | bytes 1048576 | tf_op jit(solution)/shard_map/mul | solution.py:386
  180.4 13.1 %channel.1 = (bf16[512,2048]{1,0:T(8,128)(2,1)S(1)}, f32[32,64,64]{2,1,0:T(8,128)S(1)}, f32[4,512,32]{2,1,0:T(8,128)S(1)}) custom-call(bf16[32,64,512]{2,1,0:T(8,128)(2,1)} %bitcast.60, bf16[32,64,512]{2,1,0:T(8,128)(2,1)} %bitcast.61, bf16[8,256,256]{2,1,0:T(8,128)(2,1)S(1)} %broadcast_multiply_fusion.1.w_ref, ...), custom_call_target="tpu_custom_call" | custom-call | tf_op jit(solution)/shard_map/channel/pallas_call | solution.py:349
  197.3 2.2 pad_maximum_fusion
  199.6 2.7 convolution_convert_fusion.2
  204.5 3.5 copy.49
  208.0 2.6 reshape.95.refs_0_
  210.6 114.6 %exchange.2 = (bf16[256,2,2048]{2,1,0:T(2,128)(2,1)}, bf16[256,2,2,1024]{3,2,1,0:T(2,128)(2,1)}, f32[32,8,8,128]{3,2,1,0:T(8,128)}) custom-call(bf16[256,2,2048]{2,1,0:T(2,128)(2,1)} %reshape.95.refs_0_, bf16[256,2,2,1024]{3,2,1,0:T(2,128)(2,1)} %bitcast.51, f32[32,8,8,128]{3,2,1,0:T(8,128)} %bitcast.55), custom_call_target="tpu_custom_call" | custom-call | tf_op jit(solution)/shard_map/exchange/pallas_call | solution.py:206
  325.2 4.4 fusion
  329.6 2.9 copy.25
  332.6 2.8 reshape.101
  335.3 5.3 %copy.26 = bf16[8,2,16,2,2,1024]{5,4,3,2,1,0:T(2,128)(2,1)} copy(bf16[8,2,16,2,2,1024]{5,1,2,3,0,4:T(2,128)(2,1)} %bitcast.54) | data formatting | bytes 4194304 | tf_op jit(solution)/shard_map/transpose | solution.py:411
  341.3 62.1 %exchange.3 = (bf16[256,2,2,1024]{3,2,1,0:T(2,128)(2,1)}, f32[8,8,128]{2,1,0:T(8,128)}) custom-call(bf16[256,2,2,1024]{3,2,1,0:T(2,128)(2,1)} %bitcast.52, f32[8,8,128]{2,1,0:T(8,128)} %reduce_sum.18.refs_1_), custom_call_target="tpu_custom_call" | custom-call | tf_op jit(solution)/shard_map/exchange/pallas_call | solution.py:206
  403.4 3.9 copy.27
  407.3 2.9 fusion.28
  410.3 2.7 convolution_convert_fusion.1.ret_ref
  413.6 81.9 %give_back.1 = (bf16[64,16384]{1,0:T(8,128)(2,1)}, bf16[512,512]{1,0:T(8,128)(2,1)}, f32[256,8,128]{2,1,0:T(8,128)}) custom-call(bf16[2,1024,512]{2,1,0:T(8,128)(2,1)} %convolution_convert_fusion.1.ret_ref, bf16[2,512,512]{2,1,0:T(8,128)(2,1)} %get-tuple-element.40.grad_ref, f32[8,128]{1,0:T(8,128)} %reduce_sum.19.term_ref), custom_call_target="tpu_custom_call" | custom-call | tf_op jit(solution)/shard_map/give_back/pallas_call | solution.py:281
  495.5 2.4 fusion.16
  502.0 3.9 copy.30
  506.0 2.8 reshape.105
  508.8 3.9 fusion.10
  (49 shorter events, 17.1 us)
Async XLA Ops:
  0.6 124.3 %copy-start.7 = (bf16[64,32,32]{0,2,1:T(8,128)(2,1)S(1)}, bf16[64,32,32]{0,2,1:T(8,128)(2,1)}, u32[]{:S(2)}) copy-start(bf16[64,32,32]{0,2,1:T(8,128)(2,1)} %param.13) | copy-start | bytes 393220
  175.7 1.5 copy-start.6
  197.3 2.3 copy-start.1
  210.6 114.7 %copy-start.8 = (bf16[2,256,256]{2,1,0:T(8,128)(2,1)S(1)}, bf16[2,256,256]{2,1,0:T(8,128)(2,1)}, u32[]{:S(2)}) copy-start(bf16[2,256,256]{2,1,0:T(8,128)(2,1)} %param.11) | copy-start | bytes 786436
  335.3 5.3 %copy-start.4 = (f32[32,8,8,128]{3,2,1,0:T(8,128)S(1)}, f32[32,8,8,128]{3,2,1,0:T(8,128)}, u32[]{:S(2)}) copy-start(f32[32,8,8,128]{3,2,1,0:T(8,128)} %get-tuple-element.28) | copy-start | bytes 3145732
  403.4 3.9 copy-start.2
  407.3 2.9 copy-start.10
  410.3 2.7 copy-start.9
  413.5 84.4 %copy-start = (bf16[64,16384]{1,0:T(8,128)(2,1)S(1)}, bf16[64,16384]{1,0:T(8,128)(2,1)}, u32[]{:S(2)}) copy-start(bf16[64,16384]{1,0:T(8,128)(2,1)} %g_ref.1) | copy-start | bytes 6291460
  495.5 2.5 copy-start.3
  497.9 1.8 copy-start.5

commit v2 on v0

v2 whole, which is shorter than its diff:
```python
import jax
import jax.numpy as jnp
from jax import lax
from jax.experimental import pallas as pl
from jax.experimental.pallas import tpu as pltpu
from jax.sharding import PartitionSpec as P

MESH = pl.DeviceIdType.MESH
ANY = pl.BlockSpec(memory_space=pl.ANY)
VMEM = pl.BlockSpec(memory_space=pltpu.VMEM)
NCTX, NCHAN, NDEV, HALF = 8, 32, 256, 16
BS, CB, CG, NB, D = 512, 64, 32, 256, 2048
KC = 16
F32, BF16 = jnp.float32, jnp.bfloat16
NN, NT, TN = ((1,), (0,)), ((1,), (1,)), ((0,), (0,))
LEFT, X0, X1, Y, G, RIGHT, IN0, IN1, MIX, PART1, IG0, IG1, GR, PART2, PART3, PART4, RET0, RET1, GL = range(19)
SEMS = 19


def dot(a, b, dims, precision=None):
    return lax.dot_general(a, b, (dims, ((), ())), preferred_element_type=F32, precision=precision)


def al(value, size):
    return pl.multiple_of(value * size, size)


def iota(shape, axis):
    return lax.broadcasted_iota(jnp.int32, shape, axis)


def kernel(
    x_ref, y_ref, g_ref, left_ref, right_ref, first_ref, second_ref,
    home_ref, gleft_ref, gright_ref, gfirst_ref, gsecond_ref,
    yt, gt, xp, lp, r16, inner, mg, mge, ine, parts, parts_in, part_own, part_col, part_sum, part_plane, part_all,
    ige, igx, gr, gr_in, ret, glp, glp_in,
    send, recv, local,
):
    ctx, chan = lax.axis_index("ctx"), lax.axis_index("chan")
    half, slot = chan // HALF, lax.rem(chan, HALF)
    yy, zhi, zlo, xc = ctx // 2, lax.rem(ctx, 2), chan // 8, lax.rem(chan, 8)
    me = ctx * NCHAN + chan
    group = ctx * 4 + zlo
    xq = lax.rem(xc, 4)
    inset = (xc // 4) == half
    partner = (ctx, lax.rem(chan + HALF, NCHAN))
    plane, level = yy * 8 + xc, zhi * 4 + zlo

    def linear_dev(linear):
        return (linear // NCHAN, lax.rem(linear, NCHAN))

    def remote(src, dst, index, device):
        return pltpu.make_async_remote_copy(
            src_ref=src, dst_ref=dst, send_sem=send.at[index], recv_sem=recv.at[index],
            device_id=device, device_id_type=MESH,
        )

    def finish(area, index):
        remote(area, area, index, partner).wait()

    def near(src, dst, index):
        return pltpu.make_async_copy(src, dst, local.at[index])

    barrier = pltpu.get_barrier_semaphore()

    @pl.loop(1, NDEV)
    def _(step):
        pl.semaphore_signal(
            barrier, inc=1, device_id=linear_dev(lax.rem(me + step, NDEV)), device_id_type=MESH
        )

    pl.semaphore_wait(barrier, NDEV - 1)

    def paired(part, other):
        return (
            x_ref.at[:, pl.ds(al(other + HALF * part, BS), BS)],
            xp.at[part, pl.ds(al(slot, CB), CB), :],
        )

    def whole(src, dst, peer):
        return src.at[:, pl.ds(al(peer, BS), BS)], dst.at[pl.ds(al(chan, CB), CB), :]

    remote(left_ref.at[0], lp.at[half], LEFT, partner).start()
    begin = [
        near(left_ref.at[0], lp.at[half], LEFT),
        near(*paired(0, slot), X0),
        near(*paired(1, slot), X1),
        near(*whole(y_ref, yt, chan), Y),
        near(*whole(g_ref, gt, chan), G),
        near(right_ref, r16.at[pl.ds(xc * 2, 2)], RIGHT),
    ]
    for copy in begin:
        copy.start()

    @pl.loop(1, HALF)
    def _(step):
        other = lax.rem(slot + step, HALF)
        for part in range(2):
            remote(*paired(part, other), X0 + part, (ctx, half * HALF + other)).start()

    @pl.loop(1, NCHAN)
    def _(step):
        peer = lax.rem(chan + step, NCHAN)
        remote(*whole(y_ref, yt, peer), Y, (ctx, peer)).start()

    @pl.loop(1, NCHAN)
    def _(step):
        peer = lax.rem(chan + step, NCHAN)
        remote(*whole(g_ref, gt, peer), G, (ctx, peer)).start()

    @pl.loop(1, 8)
    def _(step):
        peer = lax.rem(xc + step, 8)
        remote(right_ref, r16.at[pl.ds(xc * 2, 2)], RIGHT, (ctx, zlo * 8 + peer)).start()

    for copy in begin:
        copy.wait()

    finish(lp.at[0], LEFT)
    for part in range(2):
        finish(xp.at[part, pl.ds(0, (HALF - 1) * CB), :], X0 + part)
    keep = iota((BS, BS), 0) >= iota((BS, BS), 1)
    for part in range(2):
        lower = jnp.where(keep, lp[part], jnp.zeros((BS, BS), BF16))
        lp[part] = lower
        inner[part] = dot(lower, xp[part], NT).astype(BF16)

    def inner_to(part, other_group, quarter):
        src = inner.at[part, pl.ds(al(other_group, 16), 16), pl.ds(al(quarter, 256), 256)]
        dst = ine.at[ctx * NCHAN + slot + HALF * part]
        return src, dst, (other_group // 4, lax.rem(other_group, 4) * 8 + half * 4 + quarter)

    def channel(w, s, fs, fg, gated):
        rows4, cols4 = iota((256, 256), 0), iota((256, 256), 1)
        same = (rows4 // CB) == (cols4 // CB)
        spread4 = (lax.rem(iota((CB, 256), 1), CB) == iota((CB, 256), 0)).astype(BF16)
        for q in range(8):
            tall = first_ref[pl.ds(q * 4, 4)].reshape(256, CB)
            w[q] = jnp.where(same, dot(tall, spread4, NN), 0.0).astype(BF16)
        spread16 = (iota((CG, BS), 1) // KC == iota((CG, BS), 0)).astype(BF16)
        row, col = iota((BS, BS), 0), iota((BS, BS), 1)
        perm = (lax.rem(row, KC) * CG + row // KC == col).astype(BF16)
        for i in range(CB // KC):
            tall = second_ref[pl.ds(i * KC, KC)].reshape(BS, CG)
            wide = jnp.where(row // CG == lax.rem(col, KC), dot(tall, spread16, NN), 0.0)
            s[i] = dot(perm, wide.astype(BF16), NN).astype(BF16)

        finish(yt.at[pl.ds(0, (NCHAN - 1) * CB), :], Y)
        for q in range(8):
            section = dot(w[q], yt[pl.ds(q * 256, 256), :], NN).astype(BF16)
            fs[pl.ds(q * 4, 4)] = section.reshape(4, CB, BS)
        finish(gt.at[pl.ds(0, (NCHAN - 1) * CB), :], G)

        @pl.when(inset)
        def _():
            for part in range(2):
                src, dst, _ = inner_to(part, group, xq)
                near(src, dst, IN0 + part).start()

        @pl.when(jnp.logical_not(inset))
        def _():
            for part in range(2):
                src, dst, device = inner_to(part, group, xq)
                remote(src, dst, IN0 + part, device).start()

        @pl.loop(1, 128)
        def _(step):
            for part in range(2):
                src, dst, device = inner_to(
                    part, lax.rem(group + step // 4, 32), lax.rem(xq + step, 4)
                )
                remote(src, dst, IN0 + part, device).start()

        y3, g3 = yt.reshape(CG, CB, BS), gt.reshape(CG, CB, BS)
        lane = iota((BS, 128), 1)
        source = iota((BS, 128), 0) // KC
        second = jnp.zeros((BS, 128), F32)
        for i in range(CB // KC):
            cols = pl.ds(i * KC, KC)
            section = fs[:, cols, :].reshape(BS, BS)
            pre = dot(s[i], section, NN)
            y = y3[:, cols, :].reshape(BS, BS).astype(F32)
            g = g3[:, cols, :].reshape(BS, BS).astype(F32)
            sig = jax.nn.sigmoid(pre)
            gsig = g * sig
            gg = (gsig * y * (1.0 + pre * (1.0 - sig))).astype(BF16)
            gated[:, cols, :] = (gsig * pre).reshape(CG, KC, BS)
            fg[:, cols, :] = dot(s[i], gg, TN).astype(BF16).reshape(CG, KC, BS)
            both = dot(gg, section, NT)
            both = jnp.where(lax.rem(row, KC) == lax.rem(col, KC), both, 0.0)
            pick = (lane == source + CG * i).astype(F32)
            second += dot(both, pick, NN, lax.Precision.HIGHEST)
        parts[pl.ds(1024, 512), :] = second
        parts[pl.ds(1536, 512), :] = jnp.zeros((512, 128), F32)
        eye = (row == col).astype(BF16)
        left_lane = iota((CB, 128), 1) < CB
        for q in range(8):
            quad = pl.ds(q * 4, 4)
            fgq = fg[quad].reshape(256, BS)
            back = dot(w[q], fgq, TN)
            grad = (gated[quad].reshape(256, BS) + back).astype(BF16)
            mg[:, pl.ds(q * 256, 256)] = dot(eye, grad, NT).astype(BF16)
            pf = dot(fgq, yt[pl.ds(q * 256, 256), :], NT)
            for a in range(2):
                one = pf[a * 128 : a * 128 + CB, a * 128 : a * 128 + 128]
                two = pf[a * 128 + CB : a * 128 + 128, a * 128 : a * 128 + 128]
                parts[pl.ds((q * 2 + a) * CB, CB), :] = jnp.where(left_lane, one, two)

    pl.run_scoped(
        channel,
        pltpu.VMEM((8, 256, 256), BF16),
        pltpu.VMEM((CB // KC, BS, BS), BF16),
        pltpu.VMEM((CG, CB, BS), BF16),
        pltpu.VMEM((CG, CB, BS), BF16),
        pltpu.VMEM((CG, CB, BS), F32),
    )

    def mixed_to(peer):
        return mg.at[pl.ds(al(peer // 8, 16), 16), pl.ds(al(lax.rem(peer, 8), 256), 256)], mge.at[me]

    near(*mixed_to(me), MIX).start()

    @pl.loop(1, NDEV)
    def _(step):
        peer = lax.rem(me + step, NDEV)
        remote(*mixed_to(peer), MIX, linear_dev(peer)).start()

    def plane_dev(peer):
        return ((peer // 8) * 2 + zhi, zlo * 8 + lax.rem(peer, 8))

    def column_dev(peer):
        return (yy * 2 + peer // 4, lax.rem(peer, 4) * 8 + xc)

    def share(peer):
        return parts.at[pl.ds(al(peer, 64), 64), :], parts_in.at[plane]

    near(*share(plane), PART1).start()

    @pl.loop(1, 32)
    def _(step):
        peer = lax.rem(plane + step, 32)
        remote(*share(peer), PART1, plane_dev(peer)).start()

    near(*share(plane), PART1).wait()
    finish(parts_in.at[pl.ds(0, 31)], PART1)
    part_own[...] = jnp.sum(parts_in[...], axis=0)

    def column_share(peer):
        return part_own.at[pl.ds(al(peer, 8), 8), :], part_col.at[level]

    near(*column_share(level), PART2).start()

    @pl.loop(1, 8)
    def _(step):
        peer = lax.rem(level + step, 8)
        remote(*column_share(peer), PART2, column_dev(peer)).start()

    keep_right = iota((NB, NB), 0) >= iota((NB, NB), 1)
    finish(r16.at[pl.ds(0, 14)], RIGHT)

    def back_to(part, other_ctx, other_slot):
        src = ige.at[other_ctx * NCHAN + other_slot + HALF * part]
        dst = igx.at[part, pl.ds(al(group, 16), 16), pl.ds(al(xq, 256), 256)]
        return src, dst, (other_ctx, (xc // 4) * HALF + other_slot)

    def columns(wide0, wide1, mge_by):
        wide = (wide0, wide1)

        def unpack(ref):
            for j in range(2):
                lanes = pl.ds(j * 128, 128)
                wide[j][...] = ref[:, :, lanes].reshape(NB * 16, 128).astype(F32)

        def take(e):
            rows = pl.ds(e, NB, stride=16)
            return jnp.concatenate([w[rows, :] for w in wide], axis=1).astype(BF16)

        near(*mixed_to(me), MIX).wait()
        finish(mge.at[pl.ds(0, NDEV - 1)], MIX)
        unpack(mge)

        @pl.loop(0, 16)
        def _(e):
            mge_by[e] = take(e)

        @pl.loop(0, 16)
        def _(e):
            lower = jnp.where(keep_right, r16[e], jnp.zeros((NB, NB), BF16))
            one = dot(lower, mge_by[e], TN)
            for j in range(2):
                wide[j][pl.ds(e, NB, stride=16), :] = one[:, j * 128 : (j + 1) * 128]

        for j in range(2):
            lanes = pl.ds(j * 128, 128)
            ige[:, :, lanes] = wide[j][...].astype(BF16).reshape(NB, 16, 128)

        @pl.when(inset)
        def _():
            for part in range(2):
                src, dst, _ = back_to(part, ctx, slot)
                near(src, dst, IG0 + part).start()

        @pl.when(jnp.logical_not(inset))
        def _():
            for part in range(2):
                src, dst, device = back_to(part, ctx, slot)
                remote(src, dst, IG0 + part, device).start()

        @pl.loop(1, 128)
        def _(step):
            for part in range(2):
                src, dst, device = back_to(
                    part, lax.rem(ctx + step // HALF, NCTX), lax.rem(slot + step, HALF)
                )
                remote(src, dst, IG0 + part, device).start()

        near(*column_share(level), PART2).wait()
        finish(part_col.at[pl.ds(0, 7)], PART2)
        part_sum[...] = jnp.sum(part_col[...], axis=0)
        near(part_sum, part_plane.at[level], PART3).start()

        @pl.loop(1, 8)
        def _(step):
            peer = lax.rem(level + step, 8)
            remote(part_sum, part_plane.at[level], PART3, column_dev(peer)).start()

        @pl.when(inset)
        def _():
            for part in range(2):
                src, dst, _ = inner_to(part, group, xq)
                near(src, dst, IN0 + part).wait()
                finish(ine.at[pl.ds(0, 127)], IN0 + part)

        @pl.when(jnp.logical_not(inset))
        def _():
            for part in range(2):
                finish(ine.at[pl.ds(0, 128)], IN0 + part)

        unpack(ine)

        @pl.loop(0, 16)
        def _(e):
            one = dot(mge_by[e], take(e), NT)
            gr[e] = jnp.where(keep_right, one, 0.0).astype(BF16)

    pl.run_scoped(
        columns,
        pltpu.VMEM((NB * 16, 128), F32),
        pltpu.VMEM((NB * 16, 128), F32),
        pltpu.VMEM((16, NB, 256), BF16),
    )

    def right_to(peer):
        return gr.at[pl.ds(peer * 2, 2)], gr_in.at[xc]

    near(*right_to(xc), GR).start()

    @pl.loop(1, 8)
    def _(step):
        peer = lax.rem(xc + step, 8)
        remote(*right_to(peer), GR, (ctx, zlo * 8 + peer)).start()

    near(part_sum, part_plane.at[level], PART3).wait()
    finish(part_plane.at[pl.ds(0, 7)], PART3)
    near(part_plane, part_all.at[plane], PART4).start()

    @pl.loop(1, 32)
    def _(step):
        peer = lax.rem(plane + step, 32)
        remote(part_plane, part_all.at[plane], PART4, plane_dev(peer)).start()

    @pl.when(inset)
    def _():
        for part in range(2):
            src, dst, _ = back_to(part, ctx, slot)
            near(src, dst, IG0 + part).wait()
            finish(ige.at[pl.ds(0, 127)], IG0 + part)

    @pl.when(jnp.logical_not(inset))
    def _():
        for part in range(2):
            finish(ige.at[pl.ds(0, 128)], IG0 + part)

    def home_to(part, other):
        return (
            ret.at[part, pl.ds(al(other, CB), CB), :],
            home_ref.at[:, pl.ds(al(slot + HALF * part, BS), BS)],
        )

    for part in range(2):
        ret[part] = dot(igx[part], lp[part], TN).astype(BF16)
        near(*home_to(part, slot), RET0 + part).start()

        @pl.loop(1, HALF)
        def _(step, part=part):
            other = lax.rem(slot + step, HALF)
            remote(*home_to(part, other), RET0 + part, (ctx, half * HALF + other)).start()

    glp[...] = dot(igx[1 - half], xp[1 - half], NN).astype(BF16)
    remote(glp, glp_in, GL, partner).start()
    own = dot(igx[half], xp[half], NN)

    near(part_plane, part_all.at[plane], PART4).wait()
    finish(part_all.at[pl.ds(0, 31)], PART4)
    flat = part_all.reshape(NB * 8, 128)
    for p in range(16):
        block = flat[pl.ds(p * CB, CB), :]
        gfirst_ref[2 * p] = block[:, :CB]
        gfirst_ref[2 * p + 1] = block[:, CB:]
    for k in range(KC):
        block = flat[pl.ds(1024 + k, CG, stride=KC), :]
        for i in range(CB // KC):
            gsecond_ref[i * KC + k] = block[:, i * CG : (i + 1) * CG]

    near(*right_to(xc), GR).wait()
    finish(gr_in.at[pl.ds(0, 7)], GR)
    total = gr_in[0].astype(F32)
    for other in range(1, 8):
        total += gr_in[other].astype(F32)
    gright_ref[...] = total.astype(BF16)

    finish(glp_in, GL)
    gleft_ref[0] = jnp.where(keep, own + glp_in[...].astype(F32), 0.0).astype(BF16)
    for part in range(2):
        near(*home_to(part, slot), RET0 + part).wait()
        finish(ret.at[part, pl.ds(0, (HALF - 1) * CB), :], RET0 + part)


def on_device(inputs, mixed, grad_out, left_weight, right_weight, first_weight, second_weight):
    home, grad_left, grad_right, grad_first, grad_second = pl.pallas_call(
        kernel,
        out_shape=[
            jax.ShapeDtypeStruct((CB, NCHAN * BS), BF16),
            jax.ShapeDtypeStruct((1, BS, BS), BF16),
            jax.ShapeDtypeStruct((2, NB, NB), BF16),
            jax.ShapeDtypeStruct((CG, CB, CB), F32),
            jax.ShapeDtypeStruct((CB, CG, CG), F32),
        ],
        in_specs=[ANY] * 5 + [VMEM] * 2,
        out_specs=[ANY] + [VMEM] * 4,
        scratch_shapes=[
            pltpu.VMEM((D, BS), BF16),
            pltpu.VMEM((D, BS), BF16),
            pltpu.VMEM((2, HALF * CB, BS), BF16),
            pltpu.VMEM((2, BS, BS), BF16),
            pltpu.VMEM((16, NB, NB), BF16),
            pltpu.VMEM((2, BS, HALF * CB), BF16),
            pltpu.VMEM((BS, D), BF16),
            pltpu.VMEM((NB, 16, 256), BF16),
            pltpu.VMEM((NB, 16, 256), BF16),
            pltpu.VMEM((2048, 128), F32),
            pltpu.VMEM((32, 64, 128), F32),
            pltpu.VMEM((64, 128), F32),
            pltpu.VMEM((8, 8, 128), F32),
            pltpu.VMEM((8, 128), F32),
            pltpu.VMEM((8, 8, 128), F32),
            pltpu.VMEM((32, 8, 8, 128), F32),
            pltpu.VMEM((NB, 16, 256), BF16),
            pltpu.VMEM((2, BS, HALF * CB), BF16),
            pltpu.VMEM((16, NB, NB), BF16),
            pltpu.VMEM((8, 2, NB, NB), BF16),
            pltpu.VMEM((2, HALF * CB, BS), BF16),
            pltpu.VMEM((BS, BS), BF16),
            pltpu.VMEM((BS, BS), BF16),
            pltpu.SemaphoreType.DMA((SEMS,)),
            pltpu.SemaphoreType.DMA((SEMS,)),
            pltpu.SemaphoreType.DMA((SEMS,)),
        ],
        compiler_params=pltpu.CompilerParams(
            collective_id=1, has_side_effects=True, vmem_limit_bytes=62 * 1024 * 1024
        ),
        name="layer",
    )(inputs, mixed, grad_out, left_weight, right_weight, first_weight, second_weight)
    grad_input = (grad_out.astype(F32) + home.astype(F32)).astype(BF16)
    return (grad_input, grad_left, grad_right, grad_first, grad_second)


def solution(mesh):
    in_specs = (
        P("chan", "ctx"),
        P("chan", "ctx"),
        P("chan", "ctx"),
        P(("ctx", "chan"), None, None),
        P(("ctx", "chan"), None, None),
        P(),
        P(),
    )
    out_specs = (
        P("chan", "ctx"),
        P(("ctx", "chan"), None, None),
        P(("ctx", "chan"), None, None),
        P(),
        P(),
    )
    return jax.shard_map(
        on_device, mesh=mesh, in_specs=in_specs, out_specs=out_specs, check_vma=False
    )
```

time: 876 us -> 385 us (0.44); the launches traced: 864 us -> 385 us
  waiting for transfers between devices: 533 us -> 0 us
  Pallas kernels: 0 us -> 374 us
  local copies, waits for them, and re-layouts: 109 us -> 6.33 us
  starting transfers between devices: 101 us -> 0 us
  blocking collectives: 55.2 us -> 0 us
  matrix products: 34.5 us -> 0 us
  between operations: 14.5 us -> 0.66 us
  other arithmetic: 17.6 us -> 4.13 us
    pallas_call x0 -> x1, Pallas kernels: none -> 374 us  [on_device(): pl.pallas_call(kernel, out_shape=[jax.ShapeDtypeStruct((CB, NCHAN * BS),...]
    all_to_all x9 -> x0, waiting for transfers between devices: 270 us -> none  [the longest x2 45 us: spread(): lax.all_to_all(sectioned, 'ctx', split_axis=3, concat_axis=0, tiled=True)]
    psum x1 -> x0, waiting for transfers between devices: 263 us -> none  [on_device(): lax.psum((part_first, part_second), ('ctx', 'chan'))]
    all_to_all x9 -> x0, starting transfers between devices: 100 us -> none  [the longest x1 32.9 us: on_device(): lax.all_to_all(jnp.transpose(result_blocks, (2, 0, 1)), 'chan', split_axi...]
    all_to_all x1 -> x0, blocking collectives: 55.2 us -> none  [spread(): lax.all_to_all(sectioned, 'chan', split_axis=4, concat_axis=1, tiled=True)]
    dot_general x11 -> x0, matrix products: 34.5 us -> none  [the longest x1 7.55 us: on_device(): jnp.einsum('ctgk,kmg->ctmk', first_section, second_weight, preferred_elem...]
    unnamed x38 -> x13, local copies, waits for them, and re-layouts: 32.6 us -> 6.33 us
    reshape x6 -> x0, local copies, waits for them, and re-layouts: 22.7 us -> none  [the longest x2 9.6 us: spread(): values.reshape(1, 1, local_blocks, ranks, lanes, bsize // (ranks * lanes)...]
  transfers between devices with their start and end apart: 10 -> 0, of which waited for: 9 -> 0; matrix products, arithmetic and copies ran while one was open for 11% -> 0% of each run, Pallas kernels for 0% -> 0%
where the time goes in v2:
time: 385 us
  Pallas kernels  374 us (97%)
  local copies, waits for them, and re-layouts  6.33 us (2%)
  other arithmetic  4.13 us (1%)
    pallas_call x1, Pallas kernels, on_device(): pl.pallas_call(kernel, out_shape=[jax.ShapeDtypeStruct((CB, NCHAN * BS),...  374 us

profile of v2, /device:TPU:1, one launch (start us, length us, event | category | flops | bytes accessed | tf_op | source)
XLA Modules:
  0.0 384.7 jit_solution(10977239776544798507)
XLA Ops:
  0.6 2.5 copy.12.second_ref
  3.1 373.6 %layer.1 = (bf16[64,16384]{1,0:T(8,128)(2,1)}, bf16[1,512,512]{2,1,0:T(8,128)(2,1)}, bf16[2,256,256]{2,1,0:T(8,128)(2,1)}, f32[32,64,64]{2,1,0:T(8,128)}, f32[64,32,32]{2,1,0:T(8,128)}) custom-call(bf16[64,16384]{1,0:T(8,128)(2,1)} %x_ref.1, bf16[64,16384]{1,0:T(8,128)(2,1)} %y_ref.1, bf16[64,16384]{1,0:T(8,128)(2,1)} %g_ref.1, ...), custom_call_target="tpu_custom_call" | custom-call | tf_op jit(solution)/shard_map/layer/pallas_call | solution.py:430
  376.6 0.0 copy-start
  376.7 0.0 copy-start.2
  376.7 4.1 %add_convert_fusion = bf16[64,16384]{1,0:T(8,128)(2,1)} fusion(bf16[64,16384]{1,0:T(8,128)(2,1)} %get-tuple-element.10, bf16[64,16384]{1,0:T(8,128)(2,1)} %g_ref.1), kind=kLoop, calls=%fused_computation | loop fusion | flops 4194304 | bytes 6291456 | tf_op jit(solution)/shard_map/convert_element_type | solution.py:474
  380.8 0.0 copy-done
  380.8 0.0 copy-start.3
  380.8 0.0 copy-start.1
  380.8 1.4 copy.13
  382.2 0.0 copy-done.2
  382.2 0.8 copy.17
  383.0 0.0 copy-done.3
  383.0 0.7 copy.18
  383.7 0.0 copy-done.1
  383.7 1.0 copy.19
Async XLA Ops:
  376.6 4.2 %copy-start = (f32[64,32,32]{2,1,0:T(8,128)S(1)}, f32[64,32,32]{2,1,0:T(8,128)}, u32[]{:S(2)}) copy-start(f32[64,32,32]{2,1,0:T(8,128)} %get-tuple-element.19) | copy-start | bytes 786436
  376.7 5.5 %copy-start.2 = (bf16[1,512,512]{2,1,0:T(8,128)(2,1)S(1)}, bf16[1,512,512]{2,1,0:T(8,128)(2,1)}, u32[]{:S(2)}) copy-start(bf16[1,512,512]{2,1,0:T(8,128)(2,1)} %get-tuple-element.26) | copy-start | bytes 1572868
  380.8 2.2 copy-start.3
  380.8 2.9 copy-start.1

commit v3 on v2

--- a/solution.py
+++ b/solution.py
@@ -34,7 +34,7 @@
     home_ref, gleft_ref, gright_ref, gfirst_ref, gsecond_ref,
     yt, gt, xp, lp, r16, inner, mg, mge, ine, parts, parts_in, part_own, part_col, part_sum, part_plane, part_all,
     ige, igx, gr, gr_in, ret, glp, glp_in,
-    send, recv, local,
+    send, recv, local, ready,
 ):
     ctx, chan = lax.axis_index("ctx"), lax.axis_index("chan")
     half, slot = chan // HALF, lax.rem(chan, HALF)
@@ -63,13 +63,20 @@
 
     barrier = pltpu.get_barrier_semaphore()
 
-    @pl.loop(1, NDEV)
-    def _(step):
-        pl.semaphore_signal(
-            barrier, inc=1, device_id=linear_dev(lax.rem(me + step, NDEV)), device_id_type=MESH
-        )
-
-    pl.semaphore_wait(barrier, NDEV - 1)
+    def greet(semaphore, count, device_of):
+        @pl.loop(1, count)
+        def _(step):
+            pl.semaphore_signal(
+                semaphore, inc=1, device_id=device_of(step), device_id_type=MESH
+            )
+
+    def across(step):
+        return (lax.rem(ctx + step, NCTX), chan)
+
+    greet(barrier, NCHAN, lambda step: (ctx, lax.rem(chan + step, NCHAN)))
+    greet(barrier, NCTX, across)
+    pl.semaphore_wait(barrier, NCHAN + NCTX - 2)
+    greet(ready, NCTX, across)
 
     def paired(part, other):
         return (
@@ -80,7 +87,12 @@
     def whole(src, dst, peer):
         return src.at[:, pl.ds(al(peer, BS), BS)], dst.at[pl.ds(al(chan, CB), CB), :]
 
-    remote(left_ref.at[0], lp.at[half], LEFT, partner).start()
+    def bands(src, dst, index):
+        for band in range(4):
+            area = (pl.ds(band * 128, 128), pl.ds(0, band * 128 + 128))
+            remote(src.at[area], dst.at[area], index, partner).start()
+
+    bands(left_ref.at[0], lp.at[half], LEFT)
     begin = [
         near(left_ref.at[0], lp.at[half], LEFT),
         near(*paired(0, slot), X0),
@@ -92,31 +104,31 @@
     for copy in begin:
         copy.start()
 
-    @pl.loop(1, HALF)
-    def _(step):
-        other = lax.rem(slot + step, HALF)
-        for part in range(2):
-            remote(*paired(part, other), X0 + part, (ctx, half * HALF + other)).start()
-
     @pl.loop(1, NCHAN)
     def _(step):
-        peer = lax.rem(chan + step, NCHAN)
+        peer = lax.rem(chan + step * 11, NCHAN)
         remote(*whole(y_ref, yt, peer), Y, (ctx, peer)).start()
 
+        @pl.when(step < HALF)
+        def _():
+            other = lax.rem(slot + step, HALF)
+            for part in range(2):
+                remote(*paired(part, other), X0 + part, (ctx, half * HALF + other)).start()
+
     @pl.loop(1, NCHAN)
     def _(step):
-        peer = lax.rem(chan + step, NCHAN)
+        peer = lax.rem(chan + step * 11, NCHAN)
         remote(*whole(g_ref, gt, peer), G, (ctx, peer)).start()
 
-    @pl.loop(1, 8)
-    def _(step):
-        peer = lax.rem(xc + step, 8)
-        remote(right_ref, r16.at[pl.ds(xc * 2, 2)], RIGHT, (ctx, zlo * 8 + peer)).start()
+        @pl.when(step < 8)
+        def _():
+            other = lax.rem(xc + step, 8)
+            remote(right_ref, r16.at[pl.ds(xc * 2, 2)], RIGHT, (ctx, zlo * 8 + other)).start()
 
     for copy in begin:
         copy.wait()
 
-    finish(lp.at[0], LEFT)
+    finish(lp.at[0, pl.ds(0, 320), :], LEFT)
     for part in range(2):
         finish(xp.at[part, pl.ds(0, (HALF - 1) * CB), :], X0 + part)
     keep = iota((BS, BS), 0) >= iota((BS, BS), 1)
@@ -129,6 +141,24 @@
         src = inner.at[part, pl.ds(al(other_group, 16), 16), pl.ds(al(quarter, 256), 256)]
         dst = ine.at[ctx * NCHAN + slot + HALF * part]
         return src, dst, (other_group // 4, lax.rem(other_group, 4) * 8 + half * 4 + quarter)
+
+    def inner_send(part):
+        @pl.when(inset)
+        def _():
+            src, dst, _ = inner_to(part, group, xq)
+            near(src, dst, IN0 + part).start()
+
+        @pl.when(jnp.logical_not(inset))
+        def _():
+            src, dst, device = inner_to(part, group, xq)
+            remote(src, dst, IN0 + part, device).start()
+
+        @pl.loop(1, 128)
+        def _(step):
+            src, dst, device = inner_to(
+                part, lax.rem(group + step // 4, 32), lax.rem(xq + step, 4)
+            )
+            remote(src, dst, IN0 + part, device).start()
 
     def channel(w, s, fs, fg, gated):
         rows4, cols4 = iota((256, 256), 0), iota((256, 256), 1)
@@ -151,26 +181,8 @@
             fs[pl.ds(q * 4, 4)] = section.reshape(4, CB, BS)
         finish(gt.at[pl.ds(0, (NCHAN - 1) * CB), :], G)
 
-        @pl.when(inset)
-        def _():
-            for part in range(2):
-                src, dst, _ = inner_to(part, group, xq)
-                near(src, dst, IN0 + part).start()
-
-        @pl.when(jnp.logical_not(inset))
-        def _():
-            for part in range(2):
-                src, dst, device = inner_to(part, group, xq)
-                remote(src, dst, IN0 + part, device).start()
-
-        @pl.loop(1, 128)
-        def _(step):
-            for part in range(2):
-                src, dst, device = inner_to(
-                    part, lax.rem(group + step // 4, 32), lax.rem(xq + step, 4)
-                )
-                remote(src, dst, IN0 + part, device).start()
-
+        pl.semaphore_wait(ready, NCTX - 1)
+        inner_send(0)
         y3, g3 = yt.reshape(CG, CB, BS), gt.reshape(CG, CB, BS)
         lane = iota((BS, 128), 1)
         source = iota((BS, 128), 0) // KC
@@ -241,6 +253,7 @@
         peer = lax.rem(plane + step, 32)
         remote(*share(peer), PART1, plane_dev(peer)).start()
 
+    inner_send(1)
     near(*share(plane), PART1).wait()
     finish(parts_in.at[pl.ds(0, 31)], PART1)
     part_own[...] = jnp.sum(parts_in[...], axis=0)
@@ -257,6 +270,10 @@
 
     keep_right = iota((NB, NB), 0) >= iota((NB, NB), 1)
     finish(r16.at[pl.ds(0, 14)], RIGHT)
+
+    @pl.loop(0, 16)
+    def _(e):
+        r16[e] = jnp.where(keep_right, r16[e], jnp.zeros((NB, NB), BF16)).T
 
     def back_to(part, other_ctx, other_slot):
         src = ige.at[other_ctx * NCHAN + other_slot + HALF * part]
@@ -285,8 +302,7 @@
 
         @pl.loop(0, 16)
         def _(e):
-            lower = jnp.where(keep_right, r16[e], jnp.zeros((NB, NB), BF16))
-            one = dot(lower, mge_by[e], TN)
+            one = dot(r16[e], mge_by[e], NN)
             for j in range(2):
                 wide[j][pl.ds(e, NB, stride=16), :] = one[:, j * 128 : (j + 1) * 128]
 
@@ -294,25 +310,25 @@
             lanes = pl.ds(j * 128, 128)
             ige[:, :, lanes] = wide[j][...].astype(BF16).reshape(NB, 16, 128)
 
-        @pl.when(inset)
-        def _():
-            for part in range(2):
+        for turn in range(2):
+            part = xc // 4 if turn else 1 - xc // 4
+
+            @pl.when(inset)
+            def _(turn=turn, part=part):
                 src, dst, _ = back_to(part, ctx, slot)
-                near(src, dst, IG0 + part).start()
-
-        @pl.when(jnp.logical_not(inset))
-        def _():
-            for part in range(2):
+                near(src, dst, IG0 + turn).start()
+
+            @pl.when(jnp.logical_not(inset))
+            def _(turn=turn, part=part):
                 src, dst, device = back_to(part, ctx, slot)
-                remote(src, dst, IG0 + part, device).start()
-
-        @pl.loop(1, 128)
-        def _(step):
-            for part in range(2):
+                remote(src, dst, IG0 + turn, device).start()
+
+            @pl.loop(1, 128)
+            def _(step, turn=turn, part=part):
                 src, dst, device = back_to(
                     part, lax.rem(ctx + step // HALF, NCTX), lax.rem(slot + step, HALF)
                 )
-                remote(src, dst, IG0 + part, device).start()
+                remote(src, dst, IG0 + turn, device).start()
 
         near(*column_share(level), PART2).wait()
         finish(part_col.at[pl.ds(0, 7)], PART2)
@@ -369,35 +385,37 @@
         peer = lax.rem(plane + step, 32)
         remote(part_plane, part_all.at[plane], PART4, plane_dev(peer)).start()
 
-    @pl.when(inset)
-    def _():
-        for part in range(2):
-            src, dst, _ = back_to(part, ctx, slot)
-            near(src, dst, IG0 + part).wait()
-            finish(ige.at[pl.ds(0, 127)], IG0 + part)
-
-    @pl.when(jnp.logical_not(inset))
-    def _():
-        for part in range(2):
-            finish(ige.at[pl.ds(0, 128)], IG0 + part)
-
     def home_to(part, other):
         return (
             ret.at[part, pl.ds(al(other, CB), CB), :],
             home_ref.at[:, pl.ds(al(slot + HALF * part, BS), BS)],
         )
 
-    for part in range(2):
+    for turn in range(2):
+        part = half if turn else 1 - half
+
+        @pl.when(inset)
+        def _(turn=turn):
+            src, dst, _ = back_to(xc // 4 if turn else 1 - xc // 4, ctx, slot)
+            near(src, dst, IG0 + turn).wait()
+            finish(ige.at[pl.ds(0, 127)], IG0 + turn)
+
+        @pl.when(jnp.logical_not(inset))
+        def _(turn=turn):
+            finish(ige.at[pl.ds(0, 128)], IG0 + turn)
+
         ret[part] = dot(igx[part], lp[part], TN).astype(BF16)
-        near(*home_to(part, slot), RET0 + part).start()
+        near(*home_to(part, slot), RET0 + turn).start()
 
         @pl.loop(1, HALF)
-        def _(step, part=part):
+        def _(step, turn=turn, part=part):
             other = lax.rem(slot + step, HALF)
-            remote(*home_to(part, other), RET0 + part, (ctx, half * HALF + other)).start()
-
-    glp[...] = dot(igx[1 - half], xp[1 - half], NN).astype(BF16)
-    remote(glp, glp_in, GL, partner).start()
+            remote(*home_to(part, other), RET0 + turn, (ctx, half * HALF + other)).start()
+
+        if turn == 0:
+            glp[...] = dot(igx[part], xp[part], NN).astype(BF16)
+            bands(glp, glp_in, GL)
+
     own = dot(igx[half], xp[half], NN)
 
     near(part_plane, part_all.at[plane], PART4).wait()
@@ -419,11 +437,11 @@
         total += gr_in[other].astype(F32)
     gright_ref[...] = total.astype(BF16)
 
-    finish(glp_in, GL)
+    finish(glp_in.at[pl.ds(0, 320), :], GL)
     gleft_ref[0] = jnp.where(keep, own + glp_in[...].astype(F32), 0.0).astype(BF16)
-    for part in range(2):
-        near(*home_to(part, slot), RET0 + part).wait()
-        finish(ret.at[part, pl.ds(0, (HALF - 1) * CB), :], RET0 + part)
+    for turn in range(2):
+        near(*home_to(half if turn else 1 - half, slot), RET0 + turn).wait()
+        finish(ret.at[0, pl.ds(0, (HALF - 1) * CB), :], RET0 + turn)
 
 
 def on_device(inputs, mixed, grad_out, left_weight, right_weight, first_weight, second_weight):
@@ -465,6 +483,7 @@
             pltpu.SemaphoreType.DMA((SEMS,)),
             pltpu.SemaphoreType.DMA((SEMS,)),
             pltpu.SemaphoreType.DMA((SEMS,)),
+            pltpu.SemaphoreType.REGULAR,
         ],
         compiler_params=pltpu.CompilerParams(
             collective_id=1, has_side_effects=True, vmem_limit_bytes=62 * 1024 * 1024

time: 385 us -> 347 us (0.901)
  Pallas kernels: 374 us -> 336 us
    pallas_call x1, Pallas kernels: 374 us -> 336 us  [on_device(): pl.pallas_call(kernel, out_shape=[jax.ShapeDtypeStruct((CB, NCHAN * BS),...]
where the time goes in v3:
time: 347 us
  Pallas kernels  336 us (97%)
  local copies, waits for them, and re-layouts  6.33 us (2%)
  other arithmetic  4.13 us (1%)
    pallas_call x1, Pallas kernels, on_device(): pl.pallas_call(kernel, out_shape=[jax.ShapeDtypeStruct((CB, NCHAN * BS),...  336 us

profile of v3, /device:TPU:1, one launch (start us, length us, event | category | flops | bytes accessed | tf_op | source)
XLA Modules:
  0.0 347.3 jit_solution(569590349365071858)
XLA Ops:
  0.6 2.5 copy.12.second_ref
  3.1 336.2 %layer.1 = (bf16[64,16384]{1,0:T(8,128)(2,1)}, bf16[1,512,512]{2,1,0:T(8,128)(2,1)}, bf16[2,256,256]{2,1,0:T(8,128)(2,1)}, f32[32,64,64]{2,1,0:T(8,128)}, f32[64,32,32]{2,1,0:T(8,128)}) custom-call(bf16[64,16384]{1,0:T(8,128)(2,1)} %x_ref.1, bf16[64,16384]{1,0:T(8,128)(2,1)} %y_ref.1, bf16[64,16384]{1,0:T(8,128)(2,1)} %g_ref.1, ...), custom_call_target="tpu_custom_call" | custom-call | tf_op jit(solution)/shard_map/layer/pallas_call | solution.py:448
  339.3 0.0 copy-start
  339.3 0.0 copy-start.2
  339.3 4.1 %add_convert_fusion = bf16[64,16384]{1,0:T(8,128)(2,1)} fusion(bf16[64,16384]{1,0:T(8,128)(2,1)} %get-tuple-element.10, bf16[64,16384]{1,0:T(8,128)(2,1)} %g_ref.1), kind=kLoop, calls=%fused_computation | loop fusion | flops 4194304 | bytes 6291456 | tf_op jit(solution)/shard_map/convert_element_type | solution.py:493
  343.5 0.0 copy-done
  343.5 0.0 copy-start.3
  343.5 0.0 copy-start.1
  343.5 1.4 copy.13
  344.9 0.0 copy-done.2
  344.9 0.8 copy.17
  345.6 0.0 copy-done.3
  345.6 0.7 copy.18
  346.4 0.0 copy-done.1
  346.4 1.0 copy.19
Async XLA Ops:
  339.3 4.2 %copy-start = (f32[64,32,32]{2,1,0:T(8,128)S(1)}, f32[64,32,32]{2,1,0:T(8,128)}, u32[]{:S(2)}) copy-start(f32[64,32,32]{2,1,0:T(8,128)} %get-tuple-element.19) | copy-start | bytes 786436
  339.3 5.5 %copy-start.2 = (bf16[1,512,512]{2,1,0:T(8,128)(2,1)S(1)}, bf16[1,512,512]{2,1,0:T(8,128)(2,1)}, u32[]{:S(2)}) copy-start(bf16[1,512,512]{2,1,0:T(8,128)(2,1)} %get-tuple-element.26) | copy-start | bytes 1572868
  343.5 2.2 copy-start.3
  343.5 2.9 copy-start.1

commit v4 on v3

--- a/solution.py
+++ b/solution.py
@@ -33,21 +33,25 @@
     x_ref, y_ref, g_ref, left_ref, right_ref, first_ref, second_ref,
     home_ref, gleft_ref, gright_ref, gfirst_ref, gsecond_ref,
     yt, gt, xp, lp, r16, inner, mg, mge, ine, parts, parts_in, part_own, part_col, part_sum, part_plane, part_all,
-    ige, igx, gr, gr_in, ret, glp, glp_in,
+    ige, igx, gr, gr_in, ret, glp, glp_in, order,
     send, recv, local, ready,
 ):
     ctx, chan = lax.axis_index("ctx"), lax.axis_index("chan")
     half, slot = chan // HALF, lax.rem(chan, HALF)
     yy, zhi, zlo, xc = ctx // 2, lax.rem(ctx, 2), chan // 8, lax.rem(chan, 8)
     me = ctx * NCHAN + chan
-    group = ctx * 4 + zlo
-    xq = lax.rem(xc, 4)
-    inset = (xc // 4) == half
+    group = zhi * 16 + zlo * 4 + xc // 2
+    member = yy * 2 + lax.rem(xc, 2)
+    quarter_me = lax.rem(member, 4)
+    hq = lax.rem(member // 4 + half, 2)
+    inset = hq == half
     partner = (ctx, lax.rem(chan + HALF, NCHAN))
     plane, level = yy * 8 + xc, zhi * 4 + zlo
 
-    def linear_dev(linear):
-        return (linear // NCHAN, lax.rem(linear, NCHAN))
+    def group_dev(one_group, one_member):
+        other_ctx = one_member // 2 * 2 + one_group // 16
+        level4 = lax.rem(one_group, 16) // 4
+        return (other_ctx, level4 * 8 + lax.rem(one_group, 4) * 2 + lax.rem(one_member, 2))
 
     def remote(src, dst, index, device):
         return pltpu.make_async_remote_copy(
@@ -99,7 +103,7 @@
         near(*paired(1, slot), X1),
         near(*whole(y_ref, yt, chan), Y),
         near(*whole(g_ref, gt, chan), G),
-        near(right_ref, r16.at[pl.ds(xc * 2, 2)], RIGHT),
+        near(right_ref, r16.at[pl.ds(member * 2, 2)], RIGHT),
     ]
     for copy in begin:
         copy.start()
@@ -120,10 +124,12 @@
         peer = lax.rem(chan + step * 11, NCHAN)
         remote(*whole(g_ref, gt, peer), G, (ctx, peer)).start()
 
-        @pl.when(step < 8)
-        def _():
-            other = lax.rem(xc + step, 8)
-            remote(right_ref, r16.at[pl.ds(xc * 2, 2)], RIGHT, (ctx, zlo * 8 + other)).start()
+    pl.semaphore_wait(ready, NCTX - 1)
+
+    @pl.loop(1, 8)
+    def _(step):
+        device = group_dev(group, lax.rem(member + step, 8))
+        remote(right_ref, r16.at[pl.ds(member * 2, 2)], RIGHT, device).start()
 
     for copy in begin:
         copy.wait()
@@ -132,31 +138,38 @@
     for part in range(2):
         finish(xp.at[part, pl.ds(0, (HALF - 1) * CB), :], X0 + part)
     keep = iota((BS, BS), 0) >= iota((BS, BS), 1)
+    place, position = iota((BS, BS), 0), iota((BS, BS), 1)
+    p_group, p_member = place // 16, lax.rem(place, 16) // 2
+    owner = p_member // 2 * 64 + p_group // 16 * 32 + lax.rem(p_group, 16) // 4 * 8
+    owner += lax.rem(p_group, 4) * 2 + lax.rem(p_member, 2)
+    order[...] = (position == owner * 2 + lax.rem(place, 2)).astype(BF16)
     for part in range(2):
         lower = jnp.where(keep, lp[part], jnp.zeros((BS, BS), BF16))
+        lower = dot(order[...], lower, NN).astype(BF16)
         lp[part] = lower
         inner[part] = dot(lower, xp[part], NT).astype(BF16)
 
     def inner_to(part, other_group, quarter):
         src = inner.at[part, pl.ds(al(other_group, 16), 16), pl.ds(al(quarter, 256), 256)]
         dst = ine.at[ctx * NCHAN + slot + HALF * part]
-        return src, dst, (other_group // 4, lax.rem(other_group, 4) * 8 + half * 4 + quarter)
+        turn = lax.rem(half + lax.rem(other_group, 16) // 8, 2)
+        return src, dst, group_dev(other_group, turn * 4 + quarter)
 
     def inner_send(part):
         @pl.when(inset)
         def _():
-            src, dst, _ = inner_to(part, group, xq)
+            src, dst, _ = inner_to(part, group, quarter_me)
             near(src, dst, IN0 + part).start()
 
         @pl.when(jnp.logical_not(inset))
         def _():
-            src, dst, device = inner_to(part, group, xq)
+            src, dst, device = inner_to(part, group, quarter_me)
             remote(src, dst, IN0 + part, device).start()
 
         @pl.loop(1, 128)
         def _(step):
             src, dst, device = inner_to(
-                part, lax.rem(group + step // 4, 32), lax.rem(xq + step, 4)
+                part, lax.rem(group + step // 4, 32), lax.rem(quarter_me + step, 4)
             )
             remote(src, dst, IN0 + part, device).start()
 
@@ -167,13 +180,15 @@
         for q in range(8):
             tall = first_ref[pl.ds(q * 4, 4)].reshape(256, CB)
             w[q] = jnp.where(same, dot(tall, spread4, NN), 0.0).astype(BF16)
-        spread16 = (iota((CG, BS), 1) // KC == iota((CG, BS), 0)).astype(BF16)
         row, col = iota((BS, BS), 0), iota((BS, BS), 1)
-        perm = (lax.rem(row, KC) * CG + row // KC == col).astype(BF16)
+        sec = second_ref[...].reshape(CG * CG, CB)
+        own_out = iota((BS, CG * CG), 0) // KC == iota((BS, CG * CG), 1) // CG
+        own_in = (lax.rem(iota((CG * CG, BS), 0), CG) == iota((CG * CG, BS), 1) // KC).astype(BF16)
         for i in range(CB // KC):
-            tall = second_ref[pl.ds(i * KC, KC)].reshape(BS, CG)
-            wide = jnp.where(row // CG == lax.rem(col, KC), dot(tall, spread16, NN), 0.0)
-            s[i] = dot(perm, wide.astype(BF16), NN).astype(BF16)
+            unit = iota((BS, CB), 1) == i * KC + lax.rem(iota((BS, CB), 0), KC)
+            wide = jnp.where(own_out, dot(unit.astype(BF16), sec, NT), 0.0).astype(BF16)
+            wide = dot(wide, own_in, NN)
+            s[i] = jnp.where(lax.rem(row, KC) == lax.rem(col, KC), wide, 0.0).astype(BF16)
 
         finish(yt.at[pl.ds(0, (NCHAN - 1) * CB), :], Y)
         for q in range(8):
@@ -181,7 +196,6 @@
             fs[pl.ds(q * 4, 4)] = section.reshape(4, CB, BS)
         finish(gt.at[pl.ds(0, (NCHAN - 1) * CB), :], G)
 
-        pl.semaphore_wait(ready, NCTX - 1)
         inner_send(0)
         y3, g3 = yt.reshape(CG, CB, BS), gt.reshape(CG, CB, BS)
         lane = iota((BS, 128), 1)
@@ -204,14 +218,13 @@
             second += dot(both, pick, NN, lax.Precision.HIGHEST)
         parts[pl.ds(1024, 512), :] = second
         parts[pl.ds(1536, 512), :] = jnp.zeros((512, 128), F32)
-        eye = (row == col).astype(BF16)
         left_lane = iota((CB, 128), 1) < CB
         for q in range(8):
             quad = pl.ds(q * 4, 4)
             fgq = fg[quad].reshape(256, BS)
             back = dot(w[q], fgq, TN)
             grad = (gated[quad].reshape(256, BS) + back).astype(BF16)
-            mg[:, pl.ds(q * 256, 256)] = dot(eye, grad, NT).astype(BF16)
+            mg[:, pl.ds(q * 256, 256)] = dot(order[...], grad, NT).astype(BF16)
             pf = dot(fgq, yt[pl.ds(q * 256, 256), :], NT)
             for a in range(2):
                 one = pf[a * 128 : a * 128 + CB, a * 128 : a * 128 + 128]
@@ -228,14 +241,18 @@
     )
 
     def mixed_to(peer):
-        return mg.at[pl.ds(al(peer // 8, 16), 16), pl.ds(al(lax.rem(peer, 8), 256), 256)], mge.at[me]
-
-    near(*mixed_to(me), MIX).start()
+        other_group, other = peer // 8, lax.rem(peer, 8)
+        eighth = lax.rem(other + lax.rem(other_group, 16) // 8 * 4, 8)
+        src = mg.at[pl.ds(al(other_group, 16), 16), pl.ds(al(eighth, 256), 256)]
+        return src, mge.at[me], group_dev(other_group, other)
+
+    here = group * 8 + member
+    near(*mixed_to(here)[:2], MIX).start()
 
     @pl.loop(1, NDEV)
     def _(step):
-        peer = lax.rem(me + step, NDEV)
-        remote(*mixed_to(peer), MIX, linear_dev(peer)).start()
+        src, dst, device = mixed_to(lax.rem(here + step, NDEV))
+        remote(src, dst, MIX, device).start()
 
     def plane_dev(peer):
         return ((peer // 8) * 2 + zhi, zlo * 8 + lax.rem(peer, 8))
@@ -277,8 +294,8 @@
 
     def back_to(part, other_ctx, other_slot):
         src = ige.at[other_ctx * NCHAN + other_slot + HALF * part]
-        dst = igx.at[part, pl.ds(al(group, 16), 16), pl.ds(al(xq, 256), 256)]
-        return src, dst, (other_ctx, (xc // 4) * HALF + other_slot)
+        dst = igx.at[part, pl.ds(al(group, 16), 16), pl.ds(al(quarter_me, 256), 256)]
+        return src, dst, (other_ctx, hq * HALF + other_slot)
 
     def columns(wide0, wide1, mge_by):
         wide = (wide0, wide1)
@@ -292,15 +309,15 @@
             rows = pl.ds(e, NB, stride=16)
             return jnp.concatenate([w[rows, :] for w in wide], axis=1).astype(BF16)
 
-        near(*mixed_to(me), MIX).wait()
+        near(*mixed_to(here)[:2], MIX).wait()
         finish(mge.at[pl.ds(0, NDEV - 1)], MIX)
         unpack(mge)
 
-        @pl.loop(0, 16)
+        @pl.loop(0, 16, unroll=2)
         def _(e):
             mge_by[e] = take(e)
 
-        @pl.loop(0, 16)
+        @pl.loop(0, 16, unroll=2)
         def _(e):
             one = dot(r16[e], mge_by[e], NN)
             for j in range(2):
@@ -311,7 +328,7 @@
             ige[:, :, lanes] = wide[j][...].astype(BF16).reshape(NB, 16, 128)
 
         for turn in range(2):
-            part = xc // 4 if turn else 1 - xc // 4
+            part = hq if turn else 1 - hq
 
             @pl.when(inset)
             def _(turn=turn, part=part):
@@ -343,7 +360,7 @@
         @pl.when(inset)
         def _():
             for part in range(2):
-                src, dst, _ = inner_to(part, group, xq)
+                src, dst, _ = inner_to(part, group, quarter_me)
                 near(src, dst, IN0 + part).wait()
                 finish(ine.at[pl.ds(0, 127)], IN0 + part)
 
@@ -354,7 +371,7 @@
 
         unpack(ine)
 
-        @pl.loop(0, 16)
+        @pl.loop(0, 16, unroll=2)
         def _(e):
             one = dot(mge_by[e], take(e), NT)
             gr[e] = jnp.where(keep_right, one, 0.0).astype(BF16)
@@ -367,14 +384,14 @@
     )
 
     def right_to(peer):
-        return gr.at[pl.ds(peer * 2, 2)], gr_in.at[xc]
-
-    near(*right_to(xc), GR).start()
+        return gr.at[pl.ds(peer * 2, 2)], gr_in.at[member]
+
+    near(*right_to(member), GR).start()
 
     @pl.loop(1, 8)
     def _(step):
-        peer = lax.rem(xc + step, 8)
-        remote(*right_to(peer), GR, (ctx, zlo * 8 + peer)).start()
+        peer = lax.rem(member + step, 8)
+        remote(*right_to(peer), GR, group_dev(group, peer)).start()
 
     near(part_sum, part_plane.at[level], PART3).wait()
     finish(part_plane.at[pl.ds(0, 7)], PART3)
@@ -396,7 +413,7 @@
 
         @pl.when(inset)
         def _(turn=turn):
-            src, dst, _ = back_to(xc // 4 if turn else 1 - xc // 4, ctx, slot)
+            src, dst, _ = back_to(hq if turn else 1 - hq, ctx, slot)
             near(src, dst, IG0 + turn).wait()
             finish(ige.at[pl.ds(0, 127)], IG0 + turn)
 
@@ -404,19 +421,30 @@
         def _(turn=turn):
             finish(ige.at[pl.ds(0, 128)], IG0 + turn)
 
-        ret[part] = dot(igx[part], lp[part], TN).astype(BF16)
-        near(*home_to(part, slot), RET0 + turn).start()
-
-        @pl.loop(1, HALF)
-        def _(step, turn=turn, part=part):
-            other = lax.rem(slot + step, HALF)
-            remote(*home_to(part, other), RET0 + turn, (ctx, half * HALF + other)).start()
-
+        for step in range(4):
+            quad = lax.rem(slot // 4 + step, 4)
+            area = pl.ds(al(quad, 256), 256)
+            ret[part, area, :] = dot(igx[part, :, area], lp[part], TN).astype(BF16)
+
+            @pl.loop(0, 4)
+            def _(last, turn=turn, part=part, quad=quad):
+                other = quad * 4 + lax.rem(slot + last, 4)
+
+                @pl.when(other == slot)
+                def _():
+                    near(*home_to(part, slot), RET0 + turn).start()
+
+                @pl.when(other != slot)
+                def _():
+                    device = (ctx, half * HALF + other)
+                    remote(*home_to(part, other), RET0 + turn, device).start()
+
+        sorted_back = dot(order[...], igx[part], TN).astype(BF16)
         if turn == 0:
-            glp[...] = dot(igx[part], xp[part], NN).astype(BF16)
+            glp[...] = dot(sorted_back, xp[part], NN).astype(BF16)
             bands(glp, glp_in, GL)
-
-    own = dot(igx[half], xp[half], NN)
+        else:
+            own = dot(sorted_back, xp[part], NN)
 
     near(part_plane, part_all.at[plane], PART4).wait()
     finish(part_all.at[pl.ds(0, 31)], PART4)
@@ -430,7 +458,7 @@
         for i in range(CB // KC):
             gsecond_ref[i * KC + k] = block[:, i * CG : (i + 1) * CG]
 
-    near(*right_to(xc), GR).wait()
+    near(*right_to(member), GR).wait()
     finish(gr_in.at[pl.ds(0, 7)], GR)
     total = gr_in[0].astype(F32)
     for other in range(1, 8):
@@ -480,6 +508,7 @@
             pltpu.VMEM((2, HALF * CB, BS), BF16),
             pltpu.VMEM((BS, BS), BF16),
             pltpu.VMEM((BS, BS), BF16),
+            pltpu.VMEM((BS, BS), BF16),
             pltpu.SemaphoreType.DMA((SEMS,)),
             pltpu.SemaphoreType.DMA((SEMS,)),
             pltpu.SemaphoreType.DMA((SEMS,)),
@@ -489,7 +518,10 @@
             collective_id=1, has_side_effects=True, vmem_limit_bytes=62 * 1024 * 1024
         ),
         name="layer",
-    )(inputs, mixed, grad_out, left_weight, right_weight, first_weight, second_weight)
+    )(
+        inputs, mixed, grad_out, left_weight, right_weight, first_weight,
+        jnp.transpose(second_weight, (1, 2, 0)),
+    )
     grad_input = (grad_out.astype(F32) + home.astype(F32)).astype(BF16)
     return (grad_input, grad_left, grad_right, grad_first, grad_second)
 

time: 347 us -> 312 us (0.90)
  Pallas kernels: 336 us -> 303 us
    pallas_call x1, Pallas kernels: 336 us -> 303 us  [on_device(): pl.pallas_call(kernel, out_shape=[jax.ShapeDtypeStruct((CB, NCHAN * BS),...]
where the time goes in v4:
time: 312 us
  Pallas kernels  303 us (97%)
  other arithmetic  4.13 us (1%)
  local copies, waits for them, and re-layouts  3.87 us (1%)
    pallas_call x1, Pallas kernels, on_device(): pl.pallas_call(kernel, out_shape=[jax.ShapeDtypeStruct((CB, NCHAN * BS),...  303 us

profile of v4, /device:TPU:1, one launch (start us, length us, event | category | flops | bytes accessed | tf_op | source)
XLA Modules:
  0.0 311.7 jit_solution(5655574081165433895)
XLA Ops:
  0.6 303.0 %layer.1 = (bf16[64,16384]{1,0:T(8,128)(2,1)}, bf16[1,512,512]{2,1,0:T(8,128)(2,1)}, bf16[2,256,256]{2,1,0:T(8,128)(2,1)}, f32[32,64,64]{2,1,0:T(8,128)}, f32[64,32,32]{2,1,0:T(8,128)}) custom-call(bf16[64,16384]{1,0:T(8,128)(2,1)} %x_ref.1, bf16[64,16384]{1,0:T(8,128)(2,1)} %y_ref.1, bf16[64,16384]{1,0:T(8,128)(2,1)} %g_ref.1, ...), custom_call_target="tpu_custom_call" | custom-call | tf_op jit(solution)/shard_map/layer/pallas_call | solution.py:476
  303.7 0.0 copy-start
  303.7 0.0 copy-start.2
  303.7 4.1 %add_convert_fusion = bf16[64,16384]{1,0:T(8,128)(2,1)} fusion(bf16[64,16384]{1,0:T(8,128)(2,1)} %get-tuple-element.10, bf16[64,16384]{1,0:T(8,128)(2,1)} %g_ref.1), kind=kLoop, calls=%fused_computation | loop fusion | flops 4194304 | bytes 6291456 | tf_op jit(solution)/shard_map/convert_element_type | solution.py:525
  307.8 0.0 copy-done
  307.8 0.0 copy-start.3
  307.8 0.0 copy-start.1
  307.8 1.4 copy.12
  309.2 0.0 copy-done.2
  309.2 0.8 copy.16
  310.0 0.0 copy-done.3
  310.0 0.7 copy.17
  310.7 0.0 copy-done.1
  310.7 1.0 copy.18
Async XLA Ops:
  303.7 4.2 %copy-start = (f32[64,32,32]{2,1,0:T(8,128)S(1)}, f32[64,32,32]{2,1,0:T(8,128)}, u32[]{:S(2)}) copy-start(f32[64,32,32]{2,1,0:T(8,128)} %get-tuple-element.19) | copy-start | bytes 786436
  303.7 5.5 %copy-start.2 = (bf16[1,512,512]{2,1,0:T(8,128)(2,1)S(1)}, bf16[1,512,512]{2,1,0:T(8,128)(2,1)}, u32[]{:S(2)}) copy-start(bf16[1,512,512]{2,1,0:T(8,128)(2,1)} %get-tuple-element.26) | copy-start | bytes 1572868
  307.8 2.2 copy-start.3
  307.8 2.9 copy-start.1

commit v5 on v4

--- a/solution.py
+++ b/solution.py
@@ -240,6 +240,22 @@
         pltpu.VMEM((CG, CB, BS), F32),
     )
 
+    def plane_dev(peer):
+        return ((peer // 8) * 2 + zhi, zlo * 8 + lax.rem(peer, 8))
+
+    def column_dev(peer):
+        return (yy * 2 + peer // 4, lax.rem(peer, 4) * 8 + xc)
+
+    def share(peer):
+        return parts.at[pl.ds(al(peer, 64), 64), :], parts_in.at[plane]
+
+    near(*share(plane), PART1).start()
+
+    @pl.loop(1, 32)
+    def _(step):
+        peer = lax.rem(plane + step, 32)
+        remote(*share(peer), PART1, plane_dev(peer)).start()
+
     def mixed_to(peer):
         other_group, other = peer // 8, lax.rem(peer, 8)
         eighth = lax.rem(other + lax.rem(other_group, 16) // 8 * 4, 8)
@@ -254,23 +270,6 @@
         src, dst, device = mixed_to(lax.rem(here + step, NDEV))
         remote(src, dst, MIX, device).start()
 
-    def plane_dev(peer):
-        return ((peer // 8) * 2 + zhi, zlo * 8 + lax.rem(peer, 8))
-
-    def column_dev(peer):
-        return (yy * 2 + peer // 4, lax.rem(peer, 4) * 8 + xc)
-
-    def share(peer):
-        return parts.at[pl.ds(al(peer, 64), 64), :], parts_in.at[plane]
-
-    near(*share(plane), PART1).start()
-
-    @pl.loop(1, 32)
-    def _(step):
-        peer = lax.rem(plane + step, 32)
-        remote(*share(peer), PART1, plane_dev(peer)).start()
-
-    inner_send(1)
     near(*share(plane), PART1).wait()
     finish(parts_in.at[pl.ds(0, 31)], PART1)
     part_own[...] = jnp.sum(parts_in[...], axis=0)
@@ -285,6 +284,8 @@
         peer = lax.rem(level + step, 8)
         remote(*column_share(peer), PART2, column_dev(peer)).start()
 
+    inner_send(1)
+
     keep_right = iota((NB, NB), 0) >= iota((NB, NB), 1)
     finish(r16.at[pl.ds(0, 14)], RIGHT)
 
@@ -297,6 +298,9 @@
         dst = igx.at[part, pl.ds(al(group, 16), 16), pl.ds(al(quarter_me, 256), 256)]
         return src, dst, (other_ctx, hq * HALF + other_slot)
 
+    def right_to(peer):
+        return gr.at[pl.ds(peer * 2, 2)], gr_in.at[member]
+
     def columns(wide0, wide1, mge_by):
         wide = (wide0, wide1)
 
@@ -311,6 +315,16 @@
 
         near(*mixed_to(here)[:2], MIX).wait()
         finish(mge.at[pl.ds(0, NDEV - 1)], MIX)
+        near(*column_share(level), PART2).wait()
+        finish(part_col.at[pl.ds(0, 7)], PART2)
+        part_sum[...] = jnp.sum(part_col[...], axis=0)
+        near(part_sum, part_plane.at[level], PART3).start()
+
+        @pl.loop(1, 8)
+        def _(step):
+            peer = lax.rem(level + step, 8)
+            remote(part_sum, part_plane.at[level], PART3, column_dev(peer)).start()
+
         unpack(mge)
 
         @pl.loop(0, 16, unroll=2)
@@ -327,7 +341,7 @@
             lanes = pl.ds(j * 128, 128)
             ige[:, :, lanes] = wide[j][...].astype(BF16).reshape(NB, 16, 128)
 
-        for turn in range(2):
+        def back_send(turn):
             part = hq if turn else 1 - hq
 
             @pl.when(inset)
@@ -347,15 +361,17 @@
                 )
                 remote(src, dst, IG0 + turn, device).start()
 
-        near(*column_share(level), PART2).wait()
-        finish(part_col.at[pl.ds(0, 7)], PART2)
-        part_sum[...] = jnp.sum(part_col[...], axis=0)
-        near(part_sum, part_plane.at[level], PART3).start()
-
-        @pl.loop(1, 8)
+        back_send(0)
+        near(part_sum, part_plane.at[level], PART3).wait()
+        finish(part_plane.at[pl.ds(0, 7)], PART3)
+        near(part_plane, part_all.at[plane], PART4).start()
+
+        @pl.loop(1, 32)
         def _(step):
-            peer = lax.rem(level + step, 8)
-            remote(part_sum, part_plane.at[level], PART3, column_dev(peer)).start()
+            peer = lax.rem(plane + step, 32)
+            remote(part_plane, part_all.at[plane], PART4, plane_dev(peer)).start()
+
+        back_send(1)
 
         @pl.when(inset)
         def _():
@@ -376,6 +392,13 @@
             one = dot(mge_by[e], take(e), NT)
             gr[e] = jnp.where(keep_right, one, 0.0).astype(BF16)
 
+        near(*right_to(member), GR).start()
+
+        @pl.loop(1, 8)
+        def _(step):
+            peer = lax.rem(member + step, 8)
+            remote(*right_to(peer), GR, group_dev(group, peer)).start()
+
     pl.run_scoped(
         columns,
         pltpu.VMEM((NB * 16, 128), F32),
@@ -383,25 +406,6 @@
         pltpu.VMEM((16, NB, 256), BF16),
     )
 
-    def right_to(peer):
-        return gr.at[pl.ds(peer * 2, 2)], gr_in.at[member]
-
-    near(*right_to(member), GR).start()
-
-    @pl.loop(1, 8)
-    def _(step):
-        peer = lax.rem(member + step, 8)
-        remote(*right_to(peer), GR, group_dev(group, peer)).start()
-
-    near(part_sum, part_plane.at[level], PART3).wait()
-    finish(part_plane.at[pl.ds(0, 7)], PART3)
-    near(part_plane, part_all.at[plane], PART4).start()
-
-    @pl.loop(1, 32)
-    def _(step):
-        peer = lax.rem(plane + step, 32)
-        remote(part_plane, part_all.at[plane], PART4, plane_dev(peer)).start()
-
     def home_to(part, other):
         return (
             ret.at[part, pl.ds(al(other, CB), CB), :],
@@ -421,6 +425,8 @@
         def _(turn=turn):
             finish(ige.at[pl.ds(0, 128)], IG0 + turn)
 
+        if turn == 1:
+            bands(glp, glp_in, GL)
         for step in range(4):
             quad = lax.rem(slot // 4 + step, 4)
             area = pl.ds(al(quad, 256), 256)
@@ -442,7 +448,6 @@
         sorted_back = dot(order[...], igx[part], TN).astype(BF16)
         if turn == 0:
             glp[...] = dot(sorted_back, xp[part], NN).astype(BF16)
-            bands(glp, glp_in, GL)
         else:
             own = dot(sorted_back, xp[part], NN)
 

time: 312 us -> 304 us (0.974)
  Pallas kernels: 303 us -> 295 us
    pallas_call x1, Pallas kernels: 303 us -> 295 us  [on_device(): pl.pallas_call(kernel, out_shape=[jax.ShapeDtypeStruct((CB, NCHAN * BS),...]
where the time goes in v5:
time: 304 us
  Pallas kernels  295 us (97%)
  other arithmetic  4.13 us (1%)
  local copies, waits for them, and re-layouts  3.87 us (1%)
    pallas_call x1, Pallas kernels, on_device(): pl.pallas_call(kernel, out_shape=[jax.ShapeDtypeStruct((CB, NCHAN * BS),...  295 us

profile of v5, /device:TPU:1, one launch (start us, length us, event | category | flops | bytes accessed | tf_op | source)
XLA Modules:
  0.0 303.6 jit_solution(247153177161031127)
XLA Ops:
  0.6 294.9 %layer.1 = (bf16[64,16384]{1,0:T(8,128)(2,1)}, bf16[1,512,512]{2,1,0:T(8,128)(2,1)}, bf16[2,256,256]{2,1,0:T(8,128)(2,1)}, f32[32,64,64]{2,1,0:T(8,128)}, f32[64,32,32]{2,1,0:T(8,128)}) custom-call(bf16[64,16384]{1,0:T(8,128)(2,1)} %x_ref.1, bf16[64,16384]{1,0:T(8,128)(2,1)} %y_ref.1, bf16[64,16384]{1,0:T(8,128)(2,1)} %g_ref.1, ...), custom_call_target="tpu_custom_call" | custom-call | tf_op jit(solution)/shard_map/layer/pallas_call | solution.py:481
  295.5 0.0 copy-start
  295.5 0.0 copy-start.2
  295.5 4.1 %add_convert_fusion = bf16[64,16384]{1,0:T(8,128)(2,1)} fusion(bf16[64,16384]{1,0:T(8,128)(2,1)} %get-tuple-element.10, bf16[64,16384]{1,0:T(8,128)(2,1)} %g_ref.1), kind=kLoop, calls=%fused_computation | loop fusion | flops 4194304 | bytes 6291456 | tf_op jit(solution)/shard_map/convert_element_type | solution.py:530
  299.7 0.0 copy-done
  299.7 0.0 copy-start.3
  299.7 0.0 copy-start.1
  299.7 1.4 copy.12
  301.1 0.0 copy-done.2
  301.1 0.8 copy.16
  301.9 0.0 copy-done.3
  301.9 0.7 copy.17
  302.6 0.0 copy-done.1
  302.6 1.0 copy.18
Async XLA Ops:
  295.5 4.2 %copy-start = (f32[64,32,32]{2,1,0:T(8,128)S(1)}, f32[64,32,32]{2,1,0:T(8,128)}, u32[]{:S(2)}) copy-start(f32[64,32,32]{2,1,0:T(8,128)} %get-tuple-element.19) | copy-start | bytes 786436
  295.5 5.5 %copy-start.2 = (bf16[1,512,512]{2,1,0:T(8,128)(2,1)S(1)}, bf16[1,512,512]{2,1,0:T(8,128)(2,1)}, u32[]{:S(2)}) copy-start(bf16[1,512,512]{2,1,0:T(8,128)(2,1)} %get-tuple-element.26) | copy-start | bytes 1572868
  299.7 2.2 copy-start.3
  299.7 2.9 copy-start.1

commit v6 on v5

--- a/solution.py
+++ b/solution.py
@@ -392,13 +392,6 @@
             one = dot(mge_by[e], take(e), NT)
             gr[e] = jnp.where(keep_right, one, 0.0).astype(BF16)
 
-        near(*right_to(member), GR).start()
-
-        @pl.loop(1, 8)
-        def _(step):
-            peer = lax.rem(member + step, 8)
-            remote(*right_to(peer), GR, group_dev(group, peer)).start()
-
     pl.run_scoped(
         columns,
         pltpu.VMEM((NB * 16, 128), F32),
@@ -447,6 +440,13 @@
 
         sorted_back = dot(order[...], igx[part], TN).astype(BF16)
         if turn == 0:
+            near(*right_to(member), GR).start()
+
+            @pl.loop(1, 8)
+            def _(step):
+                peer = lax.rem(member + step, 8)
+                remote(*right_to(peer), GR, group_dev(group, peer)).start()
+
             glp[...] = dot(sorted_back, xp[part], NN).astype(BF16)
         else:
             own = dot(sorted_back, xp[part], NN)

time: 304 us -> 304 us (level)
  no operation moved by 1% of the time
where the time goes in v6:
time: 304 us
  Pallas kernels  295 us (97%)
  other arithmetic  4.13 us (1%)
  local copies, waits for them, and re-layouts  3.87 us (1%)
    pallas_call x1, Pallas kernels, on_device(): pl.pallas_call(kernel, out_shape=[jax.ShapeDtypeStruct((CB, NCHAN * BS),...  295 us

profile of v6, /device:TPU:1, one launch (start us, length us, event | category | flops | bytes accessed | tf_op | source)
XLA Modules:
  0.0 303.6 jit_solution(4042041696301418779)
XLA Ops:
  0.6 294.9 %layer.1 = (bf16[64,16384]{1,0:T(8,128)(2,1)}, bf16[1,512,512]{2,1,0:T(8,128)(2,1)}, bf16[2,256,256]{2,1,0:T(8,128)(2,1)}, f32[32,64,64]{2,1,0:T(8,128)}, f32[64,32,32]{2,1,0:T(8,128)}) custom-call(bf16[64,16384]{1,0:T(8,128)(2,1)} %x_ref.1, bf16[64,16384]{1,0:T(8,128)(2,1)} %y_ref.1, bf16[64,16384]{1,0:T(8,128)(2,1)} %g_ref.1, ...), custom_call_target="tpu_custom_call" | custom-call | tf_op jit(solution)/shard_map/layer/pallas_call | solution.py:481
  295.5 0.0 copy-start
  295.5 0.0 copy-start.2
  295.5 4.1 %add_convert_fusion = bf16[64,16384]{1,0:T(8,128)(2,1)} fusion(bf16[64,16384]{1,0:T(8,128)(2,1)} %get-tuple-element.10, bf16[64,16384]{1,0:T(8,128)(2,1)} %g_ref.1), kind=kLoop, calls=%fused_computation | loop fusion | flops 4194304 | bytes 6291456 | tf_op jit(solution)/shard_map/convert_element_type | solution.py:530
  299.7 0.0 copy-done
  299.7 0.0 copy-start.3
  299.7 0.0 copy-start.1
  299.7 1.4 copy.12
  301.1 0.0 copy-done.2
  301.1 0.8 copy.16
  301.9 0.0 copy-done.3
  301.9 0.7 copy.17
  302.6 0.0 copy-done.1
  302.6 1.0 copy.18
Async XLA Ops:
  295.5 4.2 %copy-start = (f32[64,32,32]{2,1,0:T(8,128)S(1)}, f32[64,32,32]{2,1,0:T(8,128)}, u32[]{:S(2)}) copy-start(f32[64,32,32]{2,1,0:T(8,128)} %get-tuple-element.19) | copy-start | bytes 786436
  295.5 5.5 %copy-start.2 = (bf16[1,512,512]{2,1,0:T(8,128)(2,1)S(1)}, bf16[1,512,512]{2,1,0:T(8,128)(2,1)}, u32[]{:S(2)}) copy-start(bf16[1,512,512]{2,1,0:T(8,128)(2,1)} %get-tuple-element.26) | copy-start | bytes 1572868
  299.7 2.2 copy-start.3
  299.7 2.9 copy-start.1
